TPU v7x, 32 devices: a whole 2x2x4 slice. The times are simulated.
32 devices in a mesh: section: 2 (over y), scene: 4 (over z), mp: 4 (over x, core).
Axes of the slice: x: 2, y: 2, z: 4, core: 2. Of those that a mesh axis runs over, the one named last changes fastest.
Arguments:
- dec_grad: bfloat16 [4, 8, 256, 4096], P('scene', ('section', 'mp')), may hold values from -2.109375 to 2.109375
- agent_queries: bfloat16 [4, 256, 4096], P('scene', None, ('section', 'mp')), as said below
- map_keys: bfloat16 [4, 1024, 4096], P('scene', None, ('section', 'mp')), as said below
- map_values: bfloat16 [4, 1024, 4096], P('scene', None, ('section', 'mp')), may hold values from -6 to 6
- w_out: bfloat16 [4096, 4096], P(('section', 'mp'), 'scene'), may hold values from -0.09375 to 0.09375
- block_mask: int32 [4, 2, 8], P('scene'), may hold values from 0 to 1, as said below
- agent_count: int32 [4], P('scene'), may hold values from 64 to 256
Outputs:
- d_queries: bfloat16 [4, 256, 4096], P('scene', None, ('section', 'mp'))
- d_keys: bfloat16 [4, 1024, 4096], P('scene', None, ('section', 'mp'))
- d_values: bfloat16 [4, 1024, 4096], P('scene', None, ('section', 'mp'))
- d_wout: float32 [4096, 4096], P(('section', 'mp'), 'scene')
Inputs may be any that keep to these rules, and one draw needn't show every extreme that they name: `block_mask`: every agent block of a scene sees map block 0. In each scene at most 4 map blocks are seen by some agent block, and some scene reaches 4. `agent_queries`: entries are finite and of moderate size. `map_keys`: entries are finite and of moderate size.
All inputs are finite; a program needn't handle non-finite values.
Results may differ from a plain program's by a relative error of at most 0.04.
Values may be sent and summed in bfloat16 or wider, within the bound.
A program may use at most 64 MiB of HBM per device.

v0:
```python
import math

import jax
import jax.numpy as jnp
from jax import lax
from jax.sharding import PartitionSpec as P

HEAD_DIM = 128


def attend_forward(query_heads, key_heads, value_heads, visible, scaling):
    scores = (
        jnp.einsum("qhd,khd->hqk", query_heads, key_heads, preferred_element_type=jnp.float32)
        * scaling
    )
    scores = jnp.where(visible[None], scores, -1e30)
    largest = jnp.max(scores, axis=-1, keepdims=True)
    exponent = jnp.exp(scores - largest)
    probs = exponent / jnp.sum(exponent, axis=-1, keepdims=True)
    weights = probs.astype(jnp.bfloat16)
    attended = jnp.einsum("hqk,khd->qhd", weights, value_heads, preferred_element_type=jnp.float32)
    return (probs, weights, attended)


def attend_backward(
    query_heads, key_heads, value_heads, grad_heads, probs, weights, attended, scaling
):
    delta = jnp.sum(grad_heads.astype(jnp.float32) * attended, axis=-1)
    d_values = jnp.einsum(
        "hqk,qhd->khd", weights, grad_heads, preferred_element_type=jnp.float32
    ).astype(jnp.bfloat16)
    d_probs = jnp.einsum(
        "qhd,khd->hqk", grad_heads, value_heads, preferred_element_type=jnp.float32
    )
    score_grads = (probs * (d_probs - delta.T[:, :, None])).astype(jnp.bfloat16)
    d_queries = (
        scaling
        * jnp.einsum("hqk,khd->qhd", score_grads, key_heads, preferred_element_type=jnp.float32)
    ).astype(jnp.bfloat16)
    d_keys = (
        scaling
        * jnp.einsum("hqk,qhd->khd", score_grads, query_heads, preferred_element_type=jnp.float32)
    ).astype(jnp.bfloat16)
    return (d_queries, d_keys, d_values)


def reduce_weights(attended_rounded, upstream):
    term = jnp.einsum("qh,qd->hd", attended_rounded, upstream, preferred_element_type=jnp.float32)
    return lax.psum_scatter(term, "scene", scatter_dimension=1, tiled=True)


def shards(dec_grad, agent_queries, map_keys, map_values, w_out, block_mask, agent_count):
    scaling = 1.0 / math.sqrt(HEAD_DIM)
    partial_sum = jnp.sum(dec_grad[0].astype(jnp.float32), axis=0).astype(jnp.bfloat16)
    agent_total = agent_count[0]
    token_rows = partial_sum.shape[0]
    summed = lax.psum(partial_sum, ("section", "mp")).astype(jnp.float32)
    row_keep = jnp.arange(token_rows) < agent_total
    upstream = jnp.where(row_keep[:, None], summed, 0.0).astype(jnp.bfloat16)
    proj_width = w_out.shape[0]
    d_attn = jnp.einsum(
        "td,hd->th",
        upstream,
        lax.all_gather(w_out, "scene", axis=1, tiled=True),
        preferred_element_type=jnp.float32,
    ).astype(jnp.bfloat16)
    head_count = proj_width // HEAD_DIM
    query_heads = agent_queries[0].reshape(token_rows, head_count, HEAD_DIM)
    grad_heads = d_attn.reshape(token_rows, head_count, HEAD_DIM)
    key_rows = map_keys[0]
    value_rows = map_values[0]
    mask_rows = block_mask[0]
    map_blocks = mask_rows.shape[1]
    block_size = key_rows.shape[0] // map_blocks
    visible = jnp.repeat(jnp.repeat(mask_rows == 1, block_size, axis=0), block_size, axis=1)
    key_heads = key_rows.reshape(-1, head_count, HEAD_DIM)
    value_heads = value_rows.reshape(-1, head_count, HEAD_DIM)
    probs, weights, attended = attend_forward(query_heads, key_heads, value_heads, visible, scaling)
    attended_rounded = attended.astype(jnp.bfloat16).reshape(token_rows, proj_width)
    d_queries, d_keys, d_values = attend_backward(
        query_heads, key_heads, value_heads, grad_heads, probs, weights, attended, scaling
    )
    d_wout = reduce_weights(attended_rounded, upstream)
    d_keys_out = d_keys.reshape(-1, proj_width)
    d_values_out = d_values.reshape(-1, proj_width)
    return (
        d_queries.reshape(token_rows, proj_width)[None],
        d_keys_out[None],
        d_values_out[None],
        d_wout,
    )


def solution(mesh):
    return jax.shard_map(
        shards,
        mesh=mesh,
        in_specs=(
            P("scene", ("section", "mp"), None, None),
            P("scene", None, ("section", "mp")),
            P("scene", None, ("section", "mp")),
            P("scene", None, ("section", "mp")),
            P(("section", "mp"), "scene"),
            P("scene", None, None),
            P("scene"),
        ),
        out_specs=(
            P("scene", None, ("section", "mp")),
            P("scene", None, ("section", "mp")),
            P("scene", None, ("section", "mp")),
            P(("section", "mp"), "scene"),
        ),
        check_vma=False,
    )
```

profile of v0, /device:TPU:0, one launch (start us, length us, event | category | flops | bytes accessed | tf_op | source)
XLA Modules:
  0.0 257.8 jit_solution(10037114593969919864)
XLA Ops:
  8.0 0.0 copy-start.1
  8.0 0.0 all-reduce.2.cloned.1.call-start
  8.1 0.7 all-reduce.2.cloned.1.call-update
  8.8 0.0 all-gather.2.cloned.1.call-start
  8.8 0.5 all-gather.2.cloned.1.call-update
  9.3 0.0 reduce-scatter.2.cloned.1.call-start
  10.0 0.7 compare_bitcast_fusion
  10.7 0.3 broadcast_in_dim.37
  11.1 0.8 copy.29
  11.9 1.1 copy.23
  13.0 0.5 copy.24
  13.5 0.0 copy-done.2
  13.6 0.0 copy-start.3
  13.6 1.3 copy.26
  14.9 4.6 %fusion.15 = (f32[4,256]{1,0:T(4,128)S(1)}, f32[4,256,1024]{2,1,0:T(8,128)}) fusion(pred[256,1024]{1,0:T(8,128)(4,1)} %bitcast.57, bf16[256,4,128]{0,2,1:T(8,128)(2,1)S(1)} %bitcast.52, bf16[1024,4,128]{0,2,1:T(8,128)(2,1)S(1)} %bitcast.47), kind=kOutput, calls=%fused_computation.28 | convolution fusion | flops 272630784 | bytes 5771264 | tf_op jit(solution)/shard_map/sub | solution.py:18
  19.5 3.4 %fusion.5 = bf16[4,256,1024]{2,1,0:T(8,128)(2,1)S(1)} fusion(f32[4,256,1024]{2,1,0:T(8,128)} %get-tuple-element.11, f32[4,256]{1,0:T(4,128)S(1)} %get-tuple-element.10), kind=kLoop, calls=%fused_computation.11 | loop fusion | flops 2097152 | bytes 6295552 | tf_op jit(solution)/shard_map/convert_element_type | solution.py:20
  23.0 0.0 copy-start.4
  23.0 53.6 %all-reduce.2.cloned.1.call-done = bf16[256,4096]{1,0:T(8,128)(2,1)} async-done(((bf16[256,4096]{1,0:T(8,128)(2,1)}), bf16[256,4096]{1,0:T(8,128)(2,1)}) %all-reduce.2.cloned.1.call-update) | async-done | bytes 2097168 | tf_op jit(solution)/shard_map/psum | solution.py:57
  76.6 17.6 %all-gather.2.cloned.1.call-done = bf16[512,4096]{1,0:T(8,128)(2,1)} async-done(((bf16[512,1024]{1,0:T(8,128)(2,1)}), bf16[512,4096]{1,0:T(8,128)(2,1)}) %all-gather.2.cloned.1.call-update) | async-done | bytes 4194320 | tf_op jit(solution)/shard_map/all_gather | solution.py:64
  94.2 4.8 %convolution_convert_fusion.1 = bf16[256,512]{1,0:T(8,128)(2,1)} fusion(bf16[512,4096]{1,0:T(8,128)(2,1)} %all-gather.2.cloned.1.call-done, bf16[256,4096]{1,0:T(8,128)(2,1)} %all-reduce.2.cloned.1.call-done, pred[256]{0:T(512)(128)(4,1)S(1)} %iota_compare_fusion), kind=kOutput, calls=%fused_computation.16 | convolution fusion | flops 1077018624 | bytes 6553856 | tf_op jit(solution)/shard_map/td,hd->th/dot_general | solution.py:61
  99.0 1.8 copy.25
  100.8 1.9 fusion.14
  102.7 4.5 %fusion.7 = f32[512,4096]{1,0:T(8,128)} fusion(bf16[256,512]{0,1:T(8,128)(2,1)S(1)} %bitcast.56, bf16[256,4096]{1,0:T(8,128)(2,1)S(1)} %copy-done, pred[256]{0:T(512)(128)(4,1)S(1)} %iota_compare_fusion), kind=kOutput, calls=%fused_computation.18 | convolution fusion | flops 1076887552 | bytes 10748160 | tf_op jit(solution)/shard_map/qh,qd->hd/dot_general | solution.py:48
  107.3 0.0 reduce-scatter.2.cloned.1.call-update
  107.3 1.4 convolution_convert_fusion
  108.7 1.3 copy.22
  110.0 4.1 %multiply_convert_fusion = bf16[4,256,1024]{2,1,0:T(8,128)(2,1)S(1)} fusion(bf16[256,4,128]{0,2,1:T(8,128)(2,1)} %bitcast.55, bf16[1024,4,128]{0,2,1:T(8,128)(2,1)} %bitcast.49, f32[4,256]{1,0:T(4,128)S(1)} %bitcast.60, f32[4,256,1024]{2,1,0:T(8,128)} %get-tuple-element.11, f32[4,256]{1,0:T(4,128)S(1)} %get-tuple-element.10), kind=kOutput, calls=%fused_computation.1 | convolution fusion | flops 272629760 | bytes 7610368 | tf_op jit(solution)/shard_map/qhd,khd->hqk/dot_general | solution.py:32
  114.2 0.5 multiply_convert_fusion.1
  114.7 1.3 copy.21
  116.0 2.1 fusion.6
  118.1 0.8 copy.20
  118.9 131.5 %reduce-scatter.2.cloned.1.call-done = f32[512,1024]{1,0:T(8,128)} async-done(((f32[512,4096]{1,0:T(8,128)}), f32[512,1024]{1,0:T(8,128)}) %reduce-scatter.2.cloned.1.call-update) | async-done | bytes 2097168 | tf_op jit(solution)/shard_map/reduce_scatter | solution.py:49
  (8 shorter events, 0.0 us)
Async XLA Ops:
  8.0 5.0 %copy-start.1 = (bf16[1,1024,512]{2,1,0:T(8,128)(2,1)S(1)}, bf16[1,1024,512]{2,1,0:T(8,128)(2,1)}, u32[]{:S(2)}) copy-start(bf16[1,1024,512]{2,1,0:T(8,128)(2,1)} %param.9) | copy-start | bytes 3145732
  8.0 5.5 %copy-start.2 = (bf16[1,1024,512]{2,1,0:T(8,128)(2,1)S(1)}, bf16[1,1024,512]{2,1,0:T(8,128)(2,1)}, u32[]{:S(2)}) copy-start(bf16[1,1024,512]{2,1,0:T(8,128)(2,1)} %param.10) | copy-start | bytes 3145732
  8.0 68.6 %all-reduce.2.cloned.1.call-start = ((), (), s32[]{:S(2)}) async-start(), calls=%async_computation.1 | async-start | bytes 4194304 | tf_op jit(solution)/shard_map/psum | solution.py:57
  8.8 85.4 %all-gather.2.cloned.1.call-start = ((), (), s32[]{:S(2)}) async-start(), calls=%async_computation.2 | async-start | bytes 5242880 | tf_op jit(solution)/shard_map/all_gather | solution.py:64
  9.3 241.0 %reduce-scatter.2.cloned.1.call-start = ((), (), s32[]{:S(2)}) async-start(), calls=%async_computation.3 | async-start | bytes 10485760 | tf_op jit(solution)/shard_map/reduce_scatter | solution.py:49
  13.6 6.0 %copy-start.3 = (bf16[1,1024,512]{1,2,0:T(8,128)(2,1)}, bf16[1,1024,512]{1,2,0:T(8,128)(2,1)S(1)}, u32[]{:S(2)}) copy-start(bf16[1,1024,512]{1,2,0:T(8,128)(2,1)S(1)} %copy.24) | copy-start | bytes 3145732
  23.0 77.8 %copy-start.4 = (bf16[1,1024,512]{1,2,0:T(8,128)(2,1)S(1)}, bf16[1,1024,512]{1,2,0:T(8,128)(2,1)}, u32[]{:S(2)}) copy-start(bf16[1,1024,512]{1,2,0:T(8,128)(2,1)} %copy.26) | copy-start | bytes 3145732
  100.8 2.0 copy-start
Sparse Core Ops, SparseCore 0:
  12.1 64.4 all-reduce.1
Sparse Core Ops, SparseCore 1:
  10.8 83.3 all-gather.1
  107.4 142.9 reduce-scatter.1
where the time goes:
time: 258 us
  waiting for transfers between devices  204 us (79%)
  matrix products  24 us (9%)
  between operations  16.3 us (6%)
  local copies, waits for them, and re-layouts  9.43 us (4%)
  other arithmetic  4.13 us (2%)
    reduce_scatter x1, waiting for transfers between devices, reduce_weights(): return lax.psum_scatter(term, 'scene', scatter_dimension=1, tiled=True)  131 us
    psum x1, waiting for transfers between devices, shards(): summed = lax.psum(partial_sum, ('section', 'mp')).astype(jnp.float32)  53.6 us
    all_gather x1, waiting for transfers between devices, shards(): lax.all_gather(w_out, 'scene', axis=1, tiled=True)  17.6 us
  transfers between devices with their start and end apart: 3, of which 3 were waited for; matrix products, arithmetic and copies ran while one was open for 9% of the time, Pallas kernels for 0%

commit v1 on v0

--- a/solution.py
+++ b/solution.py
@@ -1,8 +1,11 @@
+import functools
 import math
 
 import jax
 import jax.numpy as jnp
 from jax import lax
+from jax.experimental import pallas as pl
+from jax.experimental.pallas import tpu as pltpu
 from jax.sharding import PartitionSpec as P
 
 HEAD_DIM = 128
@@ -91,9 +94,361 @@
     )
 
 
+def attention_kernel(
+    scenes, dec_ref, q_ref, k_ref, v_ref, w_ref, mask_ref, count_ref,
+    dq_ref, dk_ref, dv_ref, dw_ref,
+    core_in, acc, half_in, acc_half, quarter_in, piece, up, att_all, attended, probs,
+    part_out, part_in, part_own, grads,
+    core_sem, half_sem, quarter_sem, swap_send, swap_recv, g1_send, g1_recv, g2_send, g2_recv,
+    g3_send, g3_recv, att_send, att_recv, part_send, part_recv,
+):
+    z, y, m = lax.axis_index("scene"), lax.axis_index("section"), lax.axis_index("mp")
+    x, c = lax.div(m, 2), lax.rem(m, 2)
+    core_peer, x_peer, y_peer = {"mp": m + 1 - 2 * c}, {"mp": m + 2 - 4 * x}, {"section": 1 - y}
+    rows, width = q_ref.shape[1], q_ref.shape[2]
+    half, quarter, eighth = rows // 2, rows // 4, rows // 8
+    cols = w_ref.shape[1]
+    lane = cols // 2
+    heads = width // HEAD_DIM
+    scaling = 1.0 / math.sqrt(HEAD_DIM)
+    map_blocks, q_blocks = mask_ref.shape[2], mask_ref.shape[1]
+    map_block, q_block = k_ref.shape[1] // map_blocks, rows // q_blocks
+
+    def remote(src, dst, send, recv, peer):
+        return pltpu.make_async_remote_copy(
+            src_ref=src, dst_ref=dst, send_sem=send, recv_sem=recv, device_id=peer,
+            device_id_type=pl.DeviceIdType.MESH,
+        )
+
+    def span(start, size):
+        return pl.ds(pl.multiple_of(start, size), size)
+
+    def scene_at(step):
+        return lax.rem(z + step, scenes)
+
+    barrier = pltpu.get_barrier_semaphore()
+    peers = [core_peer, x_peer, y_peer] + [{"scene": scene_at(d)} for d in range(1, scenes)]
+    for peer in peers:
+        pl.semaphore_signal(barrier, inc=1, device_id=peer, device_id_type=pl.DeviceIdType.MESH)
+    pl.semaphore_wait(barrier, len(peers))
+
+    def forward(h, carry):
+        head = span(h * HEAD_DIM, HEAD_DIM)
+        for qb in range(q_blocks):
+            block = pl.ds(qb * q_block, q_block)
+            scores = lax.dot_general(
+                q_ref[0, block, head], k_ref[0, :, head], (((1,), (1,)), ((), ())),
+                preferred_element_type=jnp.float32,
+            ) * scaling
+            hidden = jnp.concatenate(
+                [
+                    jnp.full((1, map_block), jnp.where(mask_ref[0, qb, mb] == 1, 0.0, -1e30), jnp.float32)
+                    for mb in range(map_blocks)
+                ],
+                axis=1,
+            )
+            scores = scores + hidden
+            exponent = jnp.exp(scores - jnp.max(scores, axis=-1, keepdims=True))
+            prob = exponent / jnp.sum(exponent, axis=-1, keepdims=True)
+            probs[h, block, :] = prob
+            value = jnp.dot(
+                prob.astype(jnp.bfloat16), v_ref[0, :, head], preferred_element_type=jnp.float32
+            )
+            attended[block, head] = value
+            att_all[z, block, head] = value.astype(jnp.bfloat16)
+        return carry
+
+    def add(a, b):
+        return (a.astype(jnp.float32) + b.astype(jnp.float32)).astype(jnp.bfloat16)
+
+    first = remote(
+        dec_ref.at[0, 0, span((1 - c) * half, half), :], core_in, core_sem.at[0], core_sem.at[1],
+        core_peer,
+    )
+    first.start()
+    lax.fori_loop(0, 1, forward, 0)
+    first.wait()
+    for s in range(scenes):
+        for l in range(2):
+            at = pl.ds(s * cols + l * lane, lane)
+            acc[l, :, pl.ds(s * lane, lane)] = add(
+                dec_ref[0, 0, span(c * half, half), at], core_in[:, at]
+            )
+    bits = ((x, y), (y, x))
+    order = ((x_peer, y_peer), (y_peer, x_peer))
+    copies = [
+        remote(
+            acc.at[l, span((1 - bits[l][0]) * quarter, quarter), :], half_in.at[l],
+            half_sem.at[0, l], half_sem.at[1, l], order[l][0],
+        )
+        for l in range(2)
+    ]
+    for copy in copies:
+        copy.start()
+    lax.fori_loop(1, heads, forward, 0)
+
+    def move_attended(step, wait_only):
+        for way, sign in ((0, 1), (1, -1)):
+            slot = z - sign * step
+            there = (slot >= 0) if sign == 1 else (slot < scenes)
+            onward = (z < scenes - 1) if sign == 1 else (z > 0)
+
+            @pl.when(jnp.logical_and(there, onward) if step == 0 or wait_only else there)
+            def _():
+                copy = remote(
+                    att_all.at[slot], att_all.at[slot], att_send.at[way, step], att_recv.at[slot],
+                    {"scene": z + sign},
+                )
+                if wait_only:
+                    copy.wait_send()
+                elif step == 0:
+                    copy.start()
+                else:
+                    copy.wait_recv()
+                    pl.when(onward)(lambda: copy.start())
+
+    move_attended(0, False)
+    for copy in copies:
+        copy.wait()
+    copies = []
+    for l in range(2):
+        acc_half[l] = add(acc[l, span(bits[l][0] * quarter, quarter), :], half_in[l])
+        copies.append(
+            remote(
+                acc_half.at[l, span((1 - bits[l][1]) * eighth, eighth), :], quarter_in.at[l],
+                quarter_sem.at[0, l], quarter_sem.at[1, l], order[l][1],
+            )
+        )
+        copies[l].start()
+    starts = [c * half + bits[l][0] * quarter + bits[l][1] * eighth for l in range(2)]
+    places = [span(starts[l], eighth) for l in range(2)]
+    for l in range(2):
+        copies[l].wait()
+        total = add(acc_half[l, span(bits[l][1] * eighth, eighth), :], quarter_in[l])
+        row = starts[l] + lax.broadcasted_iota(jnp.int32, total.shape, 0)
+        total = jnp.where(row < count_ref[0], total.astype(jnp.float32), 0.0).astype(jnp.bfloat16)
+        for s in range(scenes):
+            piece[s, l] = total[:, s * lane : (s + 1) * lane]
+        up[z, l, places[l], :] = piece[z, l]
+
+    def swap(d, l):
+        to = scene_at(d)
+        return remote(
+            piece.at[to, l], up.at[z, l, places[l], :], swap_send.at[d, l], swap_recv.at[d, l],
+            {"scene": to},
+        )
+
+    for d in range(1, scenes):
+        for l in range(2):
+            swap(d, l).start()
+
+    def block_of(d, l, size, lead):
+        return up.at[scene_at(scenes - d), l, span(lead, size), :]
+
+    def gather_one(d, l, sides=(g1_send, g1_recv)):
+        ref = block_of(d, l, eighth, starts[l])
+        return remote(ref, ref, sides[0].at[d, l], sides[1].at[d, l], order[l][1])
+
+    def gather_two(d, l):
+        ref = block_of(d, l, quarter, c * half + bits[l][0] * quarter)
+        return remote(ref, ref, g2_send.at[d, l], g2_recv.at[d, l], order[l][0])
+
+    def gather_three(d):
+        ref = up.at[scene_at(scenes - d), :, span(c * half, half), :]
+        return remote(ref, ref, g3_send.at[d], g3_recv.at[d], core_peer)
+
+    def landed_one(d, l):
+        other = c * half + bits[l][0] * quarter + (1 - bits[l][1]) * eighth
+        ref = block_of(d, l, eighth, other)
+        return remote(ref, ref, g1_send.at[d, l], g1_recv.at[d, l], order[l][1])
+
+    def landed_two(d, l):
+        ref = block_of(d, l, quarter, c * half + (1 - bits[l][0]) * quarter)
+        return remote(ref, ref, g2_send.at[d, l], g2_recv.at[d, l], order[l][0])
+
+    def landed_three(d):
+        ref = up.at[scene_at(scenes - d), :, span((1 - c) * half, half), :]
+        return remote(ref, ref, g3_send.at[d], g3_recv.at[d], core_peer)
+
+    def send_part(d):
+        return remote(
+            part_out.at[d], part_in.at[d], part_send.at[d], part_recv.at[d],
+            {"scene": scene_at(scenes - d)},
+        )
+
+    for t in range(scenes + 3):
+        if t < scenes:
+            for l in range(2):
+                if t > 0:
+                    remote(
+                        piece.at[0, l], up.at[scene_at(scenes - t), l, places[l], :],
+                        swap_send.at[t, l], swap_recv.at[t, l], {"scene": scene_at(t)},
+                    ).wait_recv()
+                gather_one(t, l).start()
+        if t == 1:
+            for step in range(1, scenes - 1):
+                move_attended(step, False)
+        if 0 <= t - 1 < scenes:
+            for l in range(2):
+                landed_one(t - 1, l).wait_recv()
+                gather_two(t - 1, l).start()
+        if 0 <= t - 2 < scenes:
+            for l in range(2):
+                landed_two(t - 2, l).wait_recv()
+            gather_three(t - 2).start()
+        if t >= 3:
+            d = t - 3
+            landed_three(d).wait_recv()
+            slot = scene_at(scenes - d)
+            part = sum(
+                lax.dot_general(
+                    up[slot, l], w_ref[:, l * lane : (l + 1) * lane], (((1,), (1,)), ((), ())),
+                    preferred_element_type=jnp.float32,
+                )
+                for l in range(2)
+            )
+            if d == 0:
+                part_own[...] = part
+            else:
+                part_out[d] = part.astype(jnp.bfloat16)
+                send_part(d).start()
+
+    move_attended(scenes - 1, False)
+
+    def weight_columns(tile, carry):
+        for l in range(2):
+            size = lane // 2
+            at = span(tile * size, size)
+            dw_ref[:, span(l * lane + tile * size, size)] = sum(
+                lax.dot_general(
+                    att_all[s], up[s, l, :, at], (((0,), (0,)), ((), ())),
+                    preferred_element_type=jnp.float32,
+                )
+                for s in range(scenes)
+            )
+        return carry
+
+    lax.fori_loop(0, 2, weight_columns, 0)
+
+    total = part_own[...]
+    for d in range(1, scenes):
+        send_part(d).wait_recv()
+        total = total + part_in[d].astype(jnp.float32)
+    grads[...] = total.astype(jnp.bfloat16)
+
+    def backward(h, carry):
+        head = span(h * HEAD_DIM, HEAD_DIM)
+        grad = grads[:, head]
+        prob = probs[h]
+        delta = jnp.sum(grad.astype(jnp.float32) * attended[:, head], axis=-1, keepdims=True)
+        dv_ref[0, :, head] = lax.dot_general(
+            prob.astype(jnp.bfloat16), grad, (((0,), (0,)), ((), ())),
+            preferred_element_type=jnp.float32,
+        ).astype(jnp.bfloat16)
+        d_probs = lax.dot_general(
+            grad, v_ref[0, :, head], (((1,), (1,)), ((), ())), preferred_element_type=jnp.float32
+        )
+        score_grads = (prob * (d_probs - delta)).astype(jnp.bfloat16)
+        dq_ref[0, :, head] = (
+            scaling
+            * jnp.dot(score_grads, k_ref[0, :, head], preferred_element_type=jnp.float32)
+        ).astype(jnp.bfloat16)
+        dk_ref[0, :, head] = (
+            scaling
+            * lax.dot_general(
+                score_grads, q_ref[0, :, head], (((0,), (0,)), ((), ())),
+                preferred_element_type=jnp.float32,
+            )
+        ).astype(jnp.bfloat16)
+        return carry
+
+    lax.fori_loop(0, heads, backward, 0)
+
+    for step in range(scenes - 1):
+        move_attended(step, True)
+    for d in range(scenes):
+        for l in range(2):
+            if d > 0:
+                swap(d, l).wait_send()
+            gather_one(d, l).wait_send()
+            gather_two(d, l).wait_send()
+        gather_three(d).wait_send()
+        if d > 0:
+            send_part(d).wait_send()
+
+
+def fused_shards(scenes, dec_grad, agent_queries, map_keys, map_values, w_out, block_mask, agent_count):
+    rows, width = agent_queries.shape[1:]
+    map_rows = map_keys.shape[1]
+    model = dec_grad.shape[3]
+    cols = w_out.shape[1]
+    lane, packed = cols // 2, model // 2
+    heads = width // HEAD_DIM
+    bf16, f32 = jnp.bfloat16, jnp.float32
+    vmem, smem = pl.BlockSpec(memory_space=pltpu.VMEM), pl.BlockSpec(memory_space=pltpu.SMEM)
+    dma = pltpu.SemaphoreType.DMA
+    return pl.pallas_call(
+        functools.partial(attention_kernel, scenes),
+        out_shape=(
+            jax.ShapeDtypeStruct((1, rows, width), bf16),
+            jax.ShapeDtypeStruct((1, map_rows, width), bf16),
+            jax.ShapeDtypeStruct((1, map_rows, width), bf16),
+            jax.ShapeDtypeStruct((width, cols), f32),
+        ),
+        in_specs=[vmem] * 5 + [smem] * 2,
+        out_specs=(vmem,) * 4,
+        scratch_shapes=[
+            pltpu.VMEM((rows // 2, model), bf16),
+            pltpu.VMEM((2, rows // 2, packed), bf16),
+            pltpu.VMEM((2, rows // 4, packed), bf16),
+            pltpu.VMEM((2, rows // 4, packed), bf16),
+            pltpu.VMEM((2, rows // 8, packed), bf16),
+            pltpu.VMEM((scenes, 2, rows // 8, lane), bf16),
+            pltpu.VMEM((scenes, 2, rows, lane), bf16),
+            pltpu.VMEM((scenes, rows, width), bf16),
+            pltpu.VMEM((rows, width), f32),
+            pltpu.VMEM((heads, rows, map_rows), f32),
+            pltpu.VMEM((scenes, rows, width), bf16),
+            pltpu.VMEM((scenes, rows, width), bf16),
+            pltpu.VMEM((rows, width), f32),
+            pltpu.VMEM((rows, width), bf16),
+            dma((2,)),
+            dma((2, 2)),
+            dma((2, 2)),
+            dma((scenes, 2)),
+            dma((scenes, 2)),
+            dma((scenes, 2)),
+            dma((scenes, 2)),
+            dma((scenes, 2)),
+            dma((scenes, 2)),
+            dma((scenes,)),
+            dma((scenes,)),
+            dma((2, scenes)),
+            dma((scenes,)),
+            dma((scenes,)),
+            dma((scenes,)),
+        ],
+        compiler_params=pltpu.CompilerParams(
+            collective_id=0, has_side_effects=True, vmem_limit_bytes=50 * 1024 * 1024
+        ),
+    )(dec_grad, agent_queries, map_keys, map_values, w_out, block_mask, agent_count)
+
+
 def solution(mesh):
+    scenes = mesh.shape["scene"]
+
+    def body(dec_grad, agent_queries, map_keys, map_values, w_out, block_mask, agent_count):
+        args = (dec_grad, agent_queries, map_keys, map_values, w_out, block_mask, agent_count)
+        fits = (
+            (mesh.shape["section"], mesh.shape["mp"], dec_grad.shape[1]) == (2, 4, 1)
+            and scenes >= 2
+            and dec_grad.shape[2] % 128 == 0
+            and w_out.shape[1] % 512 == 0
+        )
+        return functools.partial(fused_shards, scenes)(*args) if fits else shards(*args)
+
     return jax.shard_map(
-        shards,
+        body,
         mesh=mesh,
         in_specs=(
             P("scene", ("section", "mp"), None, None),

time: 258 us -> 80.9 us (0.31)
  waiting for transfers between devices: 204 us -> 0 us
  Pallas kernels: 0 us -> 72.4 us
  matrix products: 24 us -> 0 us
  between operations: 16.3 us -> 1.3 us
  other arithmetic: 4.13 us -> 0 us
    reduce_scatter x1 -> x0, waiting for transfers between devices: 131 us -> none  [reduce_weights(): return lax.psum_scatter(term, 'scene', scatter_dimension=1, tiled=True)]
    pallas_call x0 -> x1, Pallas kernels: none -> 72.4 us  [fused_shards(): pl.pallas_call(functools.partial(attention_kernel, scenes), out_shape=(ja...]
    psum x1 -> x0, waiting for transfers between devices: 53.6 us -> none  [shards(): summed = lax.psum(partial_sum, ('section', 'mp')).astype(jnp.float32)]
    dot_general x7 -> x0, matrix products: 19.4 us -> none  [the longest x1 4.82 us: shards(): jnp.einsum('td,hd->th', upstream, lax.all_gather(w_out, 'scene', axis=1,...]
    all_gather x1 -> x0, waiting for transfers between devices: 17.6 us -> none  [shards(): lax.all_gather(w_out, 'scene', axis=1, tiled=True)]
    sub x1 -> x0, matrix products: 4.62 us -> none  [attend_forward(): exponent = jnp.exp(scores - largest)]
    convert_element_type x1 -> x0, other arithmetic: 3.44 us -> none  [attend_forward(): weights = probs.astype(jnp.bfloat16)]
    another operation x3 -> x0, local copies, waits for them, and re-layouts: 2.95 us -> none  [the longest x1 1.33 us: shards(): value_heads = value_rows.reshape(-1, head_count, HEAD_DIM)]
  transfers between devices with their start and end apart: 3 -> 0, of which waited for: 3 -> 0; matrix products, arithmetic and copies ran while one was open for 9% -> 0% of each run, Pallas kernels for 0% -> 0%
where the time goes in v1:
time: 80.9 us; the launch traced here: 80.6 us
  Pallas kernels  72.4 us (89%)
  local copies, waits for them, and re-layouts  6.88 us (9%)
  between operations  1.3 us (2%)
    pallas_call x1, Pallas kernels, fused_shards(): pl.pallas_call(functools.partial(attention_kernel, scenes), out_shape=(ja...  72.4 us
    unnamed x12, local copies, waits for them, and re-layouts  6.88 us

profile of v1, /device:TPU:0, one launch (start us, length us, event | category | flops | bytes accessed | tf_op | source)
XLA Modules:
  0.0 80.6 jit_solution(15241065401446914229)
XLA Ops:
  1.3 0.0 copy-start
  1.3 1.2 %copy-done = bf16[1,1024,512]{2,1,0:T(8,128)(2,1)S(1)} copy-done((bf16[1,1024,512]{2,1,0:T(8,128)(2,1)S(1)}, bf16[1,1024,512]{2,1,0:T(8,128)(2,1)}, u32[]{:S(2)}) %copy-start) | copy-done | bytes 1048600
  2.5 0.0 copy-start.1
  2.5 0.9 %copy-done.1 = bf16[1,256,512]{2,1,0:T(8,128)(2,1)S(1)} copy-done((bf16[1,256,512]{2,1,0:T(8,128)(2,1)S(1)}, bf16[1,256,512]{2,1,0:T(8,128)(2,1)}, u32[]{:S(2)}) %copy-start.1) | copy-done | bytes 262168
  3.5 0.0 copy-start.2
  3.5 0.7 copy-done.2
  4.1 72.4 %shard_map.102 = (bf16[1,256,512]{2,1,0:T(8,128)(2,1)S(1)}, bf16[1,1024,512]{2,1,0:T(8,128)(2,1)S(1)}, bf16[1,1024,512]{2,1,0:T(8,128)(2,1)S(1)}, f32[512,1024]{1,0:T(8,128)}) custom-call(bf16[1,1,256,4096]{3,2,1,0:T(8,128)(2,1)} %dec_ref.1, bf16[1,256,512]{2,1,0:T(8,128)(2,1)S(1)} %copy-done.1, bf16[1,1024,512]{2,1,0:T(8,128)(2,1)S(1)} %copy-done, ...), custom_call_target="tpu_custom_call" | custom-call | tf_op jit(solution)/shard_map/pallas_call | solution.py:390
  76.6 0.7 copy.16
  77.3 0.0 copy-start.3
  77.3 1.0 %copy.17 = bf16[1,1024,512]{2,1,0:T(8,128)(2,1)} copy(bf16[1,1024,512]{2,1,0:T(8,128)(2,1)S(1)} %get-tuple-element.9) | data formatting | bytes 2097152
  78.2 1.0 %copy.18 = bf16[1,1024,512]{2,1,0:T(8,128)(2,1)} copy(bf16[1,1024,512]{2,1,0:T(8,128)(2,1)S(1)} %get-tuple-element.10) | data formatting | bytes 2097152
  79.2 0.1 copy-done.3
  79.3 1.3 %copy.19 = f32[512,1024]{1,0:T(8,128)} copy(f32[512,1024]{1,0:T(8,128)S(1)} %copy-done.3) | data formatting | bytes 4194304
Async XLA Ops:
  1.3 1.2 %copy-start = (bf16[1,1024,512]{2,1,0:T(8,128)(2,1)S(1)}, bf16[1,1024,512]{2,1,0:T(8,128)(2,1)}, u32[]{:S(2)}) copy-start(bf16[1,1024,512]{2,1,0:T(8,128)(2,1)} %k_ref.1) | copy-start | bytes 3145732
  2.5 0.9 %copy-start.1 = (bf16[1,256,512]{2,1,0:T(8,128)(2,1)S(1)}, bf16[1,256,512]{2,1,0:T(8,128)(2,1)}, u32[]{:S(2)}) copy-start(bf16[1,256,512]{2,1,0:T(8,128)(2,1)} %q_ref.1) | copy-start | bytes 786436
  3.5 0.7 copy-start.2
  77.3 2.0 %copy-start.3 = (f32[512,1024]{1,0:T(8,128)S(1)}, f32[512,1024]{1,0:T(8,128)}, u32[]{:S(2)}) copy-start(f32[512,1024]{1,0:T(8,128)} %get-tuple-element.11) | copy-start | bytes 6291460

commit v2 on v0

--- a/solution.py
+++ b/solution.py
@@ -1,8 +1,11 @@
+import functools
 import math
 
 import jax
 import jax.numpy as jnp
 from jax import lax
+from jax.experimental import pallas as pl
+from jax.experimental.pallas import tpu as pltpu
 from jax.sharding import PartitionSpec as P
 
 HEAD_DIM = 128
@@ -91,9 +94,440 @@
     )
 
 
+def attention_kernel(
+    scenes, dec_hbm, q_hbm, k_hbm, v_hbm, w_hbm, mask_ref, count_ref,
+    dq_hbm, dk_hbm, dv_hbm, dw_hbm,
+    dec_ref, q_ref, k_ref, v_ref, w_ref, dq_ref, dk_ref, dv_ref, dw_ref,
+    core_in, acc, half_in, acc_half, quarter_in, piece, up, att_all, attended, probs,
+    parts, part_out, part_in, part_own, grads,
+    load_sem, store_sem, core_send, core_recv, half_send, half_recv, quarter_send, quarter_recv,
+    swap_send, swap_recv, g1_send, g1_recv, g2_send, g2_recv,
+    g3_send, g3_recv, att_send, att_recv, part_send, part_recv,
+):
+    z, y, m = lax.axis_index("scene"), lax.axis_index("section"), lax.axis_index("mp")
+    x, c = lax.div(m, 2), lax.rem(m, 2)
+    core_peer, x_peer, y_peer = {"mp": m + 1 - 2 * c}, {"mp": m + 2 - 4 * x}, {"section": 1 - y}
+    rows, width = q_ref.shape[1], q_ref.shape[2]
+    half, quarter, eighth = rows // 2, rows // 4, rows // 8
+    cols = w_ref.shape[1]
+    lane = cols // 2
+    heads = width // HEAD_DIM
+    scaling = 1.0 / math.sqrt(HEAD_DIM)
+    map_blocks, q_blocks = mask_ref.shape[2], mask_ref.shape[1]
+    map_block, q_block = k_ref.shape[1] // map_blocks, rows // q_blocks
+
+    def remote(src, dst, send, recv, peer):
+        return pltpu.make_async_remote_copy(
+            src_ref=src, dst_ref=dst, send_sem=send, recv_sem=recv, device_id=peer,
+            device_id_type=pl.DeviceIdType.MESH,
+        )
+
+    def span(start, size):
+        return pl.ds(pl.multiple_of(start, size), size)
+
+    def partner(r):
+        high, low = lax.div(z, 2), lax.rem(z, 2)
+        return 2 * (1 - high if r & 2 else high) + (1 - low if r & 1 else low)
+
+    rounds = [r for r in range(scenes - 1, -1, -1)]
+    targets = [partner(r) for r in rounds]
+
+    loads = [
+        pltpu.make_async_copy(src, dst, load_sem.at[i])
+        for i, (src, dst) in enumerate(
+            (
+                (q_hbm, q_ref), (k_hbm, k_ref), (v_hbm, v_ref), (w_hbm, w_ref),
+                (dec_hbm.at[0, 0, span(c * half, half), :], dec_ref),
+            )
+        )
+    ]
+    for load in loads:
+        load.start()
+
+    barrier = pltpu.get_barrier_semaphore()
+    peers = [core_peer, x_peer, y_peer] + [{"scene": targets[j]} for j in range(scenes - 1)]
+    for peer in peers:
+        pl.semaphore_signal(barrier, inc=1, device_id=peer, device_id_type=pl.DeviceIdType.MESH)
+    pl.semaphore_wait(barrier, len(peers))
+
+    def core_copy(j):
+        return remote(
+            dec_hbm.at[0, 0, span((1 - c) * half, half), span(targets[j] * cols, cols)],
+            core_in.at[j], core_send.at[j], core_recv.at[j], core_peer,
+        )
+
+    for j in range(scenes):
+        core_copy(j).start()
+
+    def forward(h, carry):
+        head = span(h * HEAD_DIM, HEAD_DIM)
+        for qb in range(q_blocks):
+            block = pl.ds(qb * q_block, q_block)
+            scores = lax.dot_general(
+                q_ref[0, block, head], k_ref[0, :, head], (((1,), (1,)), ((), ())),
+                preferred_element_type=jnp.float32,
+            ) * scaling
+            hidden = jnp.concatenate(
+                [
+                    jnp.full((1, map_block), jnp.where(mask_ref[0, qb, mb] == 1, 0.0, -1e30), jnp.float32)
+                    for mb in range(map_blocks)
+                ],
+                axis=1,
+            )
+            scores = scores + hidden
+            exponent = jnp.exp(scores - jnp.max(scores, axis=-1, keepdims=True))
+            prob = exponent / jnp.sum(exponent, axis=-1, keepdims=True)
+            probs[h, block, :] = prob
+            value = jnp.dot(
+                prob.astype(jnp.bfloat16), v_ref[0, :, head], preferred_element_type=jnp.float32
+            )
+            attended[block, head] = value
+            att_all[z, block, head] = value.astype(jnp.bfloat16)
+        return carry
+
+    def add(a, b):
+        return (a.astype(jnp.float32) + b.astype(jnp.float32)).astype(jnp.bfloat16)
+
+    def move_attended(step, wait_only):
+        for way, sign in ((0, 1), (1, -1)):
+            slot = z - sign * step
+            there = (slot >= 0) if sign == 1 else (slot < scenes)
+            onward = (z < scenes - 1) if sign == 1 else (z > 0)
+
+            @pl.when(jnp.logical_and(there, onward) if step == 0 or wait_only else there)
+            def _():
+                copy = remote(
+                    att_all.at[slot], att_all.at[slot], att_send.at[way, step], att_recv.at[slot],
+                    {"scene": z + sign},
+                )
+                if wait_only:
+                    copy.wait_send()
+                elif step == 0:
+                    copy.start()
+                else:
+                    copy.wait_recv()
+                    pl.when(onward)(lambda: copy.start())
+
+    bits = ((x, y), (y, x))
+    order = ((x_peer, y_peer), (y_peer, x_peer))
+    starts = [c * half + bits[l][0] * quarter + bits[l][1] * eighth for l in range(2)]
+    places = [span(starts[l], eighth) for l in range(2)]
+
+    def half_copy(j, l):
+        return remote(
+            acc.at[j, l, span((1 - bits[l][0]) * quarter, quarter), :], half_in.at[j, l],
+            half_send.at[j, l], half_recv.at[j, l], order[l][0],
+        )
+
+    def quarter_copy(j, l):
+        return remote(
+            acc_half.at[j, l, span((1 - bits[l][1]) * eighth, eighth), :], quarter_in.at[j, l],
+            quarter_send.at[j, l], quarter_recv.at[j, l], order[l][1],
+        )
+
+    def swap(j, l, slot):
+        return remote(
+            piece.at[j, l], up.at[slot, l, places[l], :], swap_send.at[j, l], swap_recv.at[j, l],
+            {"scene": targets[j]},
+        )
+
+    def sum_core(j):
+        core_copy(j).wait_recv()
+        for l in range(2):
+            mine = dec_ref[:, span(targets[j] * cols + l * lane, lane)]
+            acc[j, l] = add(mine, core_in[j, :, l * lane : (l + 1) * lane])
+            half_copy(j, l).start()
+
+    def sum_half(j):
+        for l in range(2):
+            half_copy(j, l).wait_recv()
+            acc_half[j, l] = add(acc[j, l, span(bits[l][0] * quarter, quarter), :], half_in[j, l])
+            quarter_copy(j, l).start()
+
+    def sum_quarter(j):
+        for l in range(2):
+            quarter_copy(j, l).wait_recv()
+            total = add(acc_half[j, l, span(bits[l][1] * eighth, eighth), :], quarter_in[j, l])
+            row = starts[l] + lax.broadcasted_iota(jnp.int32, total.shape, 0)
+            total = jnp.where(row < count_ref[0], total.astype(jnp.float32), 0.0)
+            if j < scenes - 1:
+                piece[j, l] = total.astype(jnp.bfloat16)
+                swap(j, l, z).start()
+            else:
+                up[z, l, places[l], :] = total.astype(jnp.bfloat16)
+
+    def gathered(j, l, size, lead, sems, peer):
+        ref = up.at[targets[j], l, span(lead, size), :]
+        return remote(ref, ref, sems[0].at[j, l], sems[1].at[j, l], peer)
+
+    def gather_one(j, l, away=0):
+        bit = 1 - bits[l][1] if away else bits[l][1]
+        lead = c * half + bits[l][0] * quarter + bit * eighth
+        return gathered(j, l, eighth, lead, (g1_send, g1_recv), order[l][1])
+
+    def gather_two(j, l, away=0):
+        bit = 1 - bits[l][0] if away else bits[l][0]
+        return gathered(j, l, quarter, c * half + bit * quarter, (g2_send, g2_recv), order[l][0])
+
+    def gather_three(j, away=0):
+        core = 1 - c if away else c
+        ref = up.at[targets[j], :, span(core * half, half), :]
+        return remote(ref, ref, g3_send.at[j], g3_recv.at[j], core_peer)
+
+    def spread_one(j):
+        for l in range(2):
+            if j < scenes - 1:
+                swap(j, l, targets[j]).wait_recv()
+            gather_one(j, l).start()
+
+    def spread_two(j):
+        for l in range(2):
+            gather_one(j, l, 1).wait_recv()
+            gather_two(j, l).start()
+
+    def spread_three(j):
+        for l in range(2):
+            gather_two(j, l, 1).wait_recv()
+        gather_three(j).start()
+
+    def part_copy(j):
+        t = targets[j]
+        to = z + jnp.where(t > z, 1, -1)
+        slot = jnp.where(jnp.logical_and(to == t, t < z), scenes, t)
+        return remote(
+            part_out.at[j], part_in.at[slot], part_send.at[j], part_recv.at[slot], {"scene": to}
+        )
+
+    def landed_part(slot):
+        return remote(
+            part_out.at[0], part_in.at[slot], part_send.at[0], part_recv.at[slot], core_peer
+        )
+
+    inner = jnp.logical_and(z > 0, z < scenes - 1)
+    has_prev = [jnp.where(targets[j] > z, z, scenes - 1 - z) > 0 for j in range(scenes)]
+
+    def multiply(j):
+        gather_three(j, 1).wait_recv()
+        t = targets[j]
+        part = sum(
+            lax.dot_general(
+                up[t, l], w_ref[:, l * lane : (l + 1) * lane], (((1,), (1,)), ((), ())),
+                preferred_element_type=jnp.float32,
+            )
+            for l in range(2)
+        )
+        if j == scenes - 1:
+            part_own[...] = part
+            return
+        parts[j] = part
+
+        @pl.when(jnp.logical_not(has_prev[j]))
+        def _():
+            part_out[j] = parts[j].astype(jnp.bfloat16)
+            part_copy(j).start()
+
+    def merge(j):
+        @pl.when(has_prev[j])
+        def _():
+            landed_part(targets[j]).wait_recv()
+            part_out[j] = (parts[j] + part_in[targets[j]].astype(jnp.float32)).astype(jnp.bfloat16)
+            part_copy(j).start()
+
+    stages = (
+        sum_core, sum_half, sum_quarter, spread_one, spread_two, spread_three, multiply
+    )
+    loads[0].wait()
+    loads[1].wait()
+    loads[2].wait()
+    forward(0, 0)
+    loads[4].wait()
+    for tick in range(scenes + len(stages) - 1):
+        for lag, stage in enumerate(stages):
+            if stage is multiply and tick == lag:
+                loads[3].wait()
+            if 0 <= tick - lag < scenes:
+                stage(tick - lag)
+        if tick + 1 < heads:
+            forward(tick + 1, 0)
+        if tick == heads - 2:
+            move_attended(0, False)
+        if tick == 5:
+            move_attended(1, False)
+        if tick == 7:
+            move_attended(2, False)
+        if tick == 8:
+            merge(1)
+        if tick == 9:
+            merge(0)
+    move_attended(scenes - 1, False)
+
+    def weight_columns(tile, carry):
+        for l in range(2):
+            size = lane // 2
+            at = span(tile * size, size)
+            dw_ref[:, span(l * lane + tile * size, size)] = sum(
+                lax.dot_general(
+                    att_all[s], up[s, l, :, at], (((0,), (0,)), ((), ())),
+                    preferred_element_type=jnp.float32,
+                )
+                for s in range(scenes)
+            )
+        return carry
+
+    lax.fori_loop(0, 2, weight_columns, 0)
+
+    store_dw = pltpu.make_async_copy(dw_ref, dw_hbm, store_sem.at[0])
+    store_dw.start()
+    merge(2)
+
+    @pl.when(z > 0)
+    def _():
+        landed_part(z).wait_recv()
+        part_own[...] = part_own[...] + part_in[z].astype(jnp.float32)
+
+    @pl.when(z < scenes - 1)
+    def _():
+        landed_part(scenes).wait_recv()
+        part_own[...] = part_own[...] + part_in[scenes].astype(jnp.float32)
+
+    grads[...] = part_own[...].astype(jnp.bfloat16)
+
+    def stores(h):
+        head = span(h * HEAD_DIM, HEAD_DIM)
+        return [
+            pltpu.make_async_copy(src.at[0, :, head], dst.at[0, :, head], store_sem.at[1 + 3 * h + i])
+            for i, (src, dst) in enumerate(((dq_ref, dq_hbm), (dk_ref, dk_hbm), (dv_ref, dv_hbm)))
+        ]
+
+    def backward(h, carry):
+        head = span(h * HEAD_DIM, HEAD_DIM)
+        grad = grads[:, head]
+        prob = probs[h]
+        delta = jnp.sum(grad.astype(jnp.float32) * attended[:, head], axis=-1, keepdims=True)
+        dv_ref[0, :, head] = lax.dot_general(
+            prob.astype(jnp.bfloat16), grad, (((0,), (0,)), ((), ())),
+            preferred_element_type=jnp.float32,
+        ).astype(jnp.bfloat16)
+        d_probs = lax.dot_general(
+            grad, v_ref[0, :, head], (((1,), (1,)), ((), ())), preferred_element_type=jnp.float32
+        )
+        score_grads = (prob * (d_probs - delta)).astype(jnp.bfloat16)
+        dq_ref[0, :, head] = (
+            scaling
+            * jnp.dot(score_grads, k_ref[0, :, head], preferred_element_type=jnp.float32)
+        ).astype(jnp.bfloat16)
+        dk_ref[0, :, head] = (
+            scaling
+            * lax.dot_general(
+                score_grads, q_ref[0, :, head], (((0,), (0,)), ((), ())),
+                preferred_element_type=jnp.float32,
+            )
+        ).astype(jnp.bfloat16)
+        return carry
+
+    for h in range(heads):
+        backward(h, 0)
+        for store in stores(h):
+            store.start()
+
+    for step in range(scenes - 1):
+        move_attended(step, True)
+    for j in range(scenes):
+        core_copy(j).wait_send()
+        for l in range(2):
+            half_copy(j, l).wait_send()
+            quarter_copy(j, l).wait_send()
+            gather_one(j, l).wait_send()
+            gather_two(j, l).wait_send()
+            if j < scenes - 1:
+                swap(j, l, z).wait_send()
+        gather_three(j).wait_send()
+        if j < scenes - 1:
+            part_copy(j).wait_send()
+    store_dw.wait()
+    for h in range(heads):
+        for store in stores(h):
+            store.wait()
+
+
+def fused_shards(scenes, dec_grad, agent_queries, map_keys, map_values, w_out, block_mask, agent_count):
+    rows, width = agent_queries.shape[1:]
+    map_rows = map_keys.shape[1]
+    model = dec_grad.shape[3]
+    cols = w_out.shape[1]
+    lane = cols // 2
+    heads = width // HEAD_DIM
+    bf16, f32 = jnp.bfloat16, jnp.float32
+    anywhere, smem = pl.BlockSpec(memory_space=pl.ANY), pl.BlockSpec(memory_space=pltpu.SMEM)
+    dma, vmem = pltpu.SemaphoreType.DMA, pltpu.VMEM
+    return pl.pallas_call(
+        functools.partial(attention_kernel, scenes),
+        out_shape=(
+            jax.ShapeDtypeStruct((1, rows, width), bf16),
+            jax.ShapeDtypeStruct((1, map_rows, width), bf16),
+            jax.ShapeDtypeStruct((1, map_rows, width), bf16),
+            jax.ShapeDtypeStruct((width, cols), f32),
+        ),
+        in_specs=[anywhere] * 5 + [smem] * 2,
+        out_specs=(anywhere,) * 4,
+        scratch_shapes=[
+            vmem((rows // 2, model), bf16),
+            vmem((1, rows, width), bf16),
+            vmem((1, map_rows, width), bf16),
+            vmem((1, map_rows, width), bf16),
+            vmem((width, cols), bf16),
+            vmem((1, rows, width), bf16),
+            vmem((1, map_rows, width), bf16),
+            vmem((1, map_rows, width), bf16),
+            vmem((width, cols), f32),
+            vmem((scenes, rows // 2, cols), bf16),
+            vmem((scenes, 2, rows // 2, lane), bf16),
+            vmem((scenes, 2, rows // 4, lane), bf16),
+            vmem((scenes, 2, rows // 4, lane), bf16),
+            vmem((scenes, 2, rows // 8, lane), bf16),
+            vmem((scenes, 2, rows // 8, lane), bf16),
+            vmem((scenes, 2, rows, lane), bf16),
+            vmem((scenes, rows, width), bf16),
+            vmem((rows, width), f32),
+            vmem((heads, rows, map_rows), f32),
+            vmem((scenes, rows, width), f32),
+            vmem((scenes, rows, width), bf16),
+            vmem((scenes + 1, rows, width), bf16),
+            vmem((rows, width), f32),
+            vmem((rows, width), bf16),
+            dma((5,)),
+            dma((1 + 3 * heads,)),
+            dma((scenes,)),
+            dma((scenes,)),
+            *[dma((scenes, 2))] * 10,
+            dma((scenes,)),
+            dma((scenes,)),
+            dma((2, scenes)),
+            dma((scenes,)),
+            dma((scenes,)),
+            dma((scenes + 1,)),
+        ],
+        compiler_params=pltpu.CompilerParams(
+            collective_id=0, has_side_effects=True, vmem_limit_bytes=52 * 1024 * 1024
+        ),
+    )(dec_grad, agent_queries, map_keys, map_values, w_out, block_mask, agent_count)
+
+
 def solution(mesh):
+    scenes = mesh.shape["scene"]
+
+    def body(dec_grad, agent_queries, map_keys, map_values, w_out, block_mask, agent_count):
+        args = (dec_grad, agent_queries, map_keys, map_values, w_out, block_mask, agent_count)
+        fits = (
+            (mesh.shape["section"], mesh.shape["mp"], dec_grad.shape[1]) == (2, 4, 1)
+            and scenes == 4
+            and dec_grad.shape[2] % 128 == 0
+            and w_out.shape[1] % 512 == 0
+        )
+        return functools.partial(fused_shards, scenes)(*args) if fits else shards(*args)
+
     return jax.shard_map(
-        shards,
+        body,
         mesh=mesh,
         in_specs=(
             P("scene", ("section", "mp"), None, None),

time: 258 us -> 67.2 us (0.26)
  waiting for transfers between devices: 204 us -> 0 us
  Pallas kernels: 0 us -> 59.9 us
  matrix products: 24 us -> 0 us
  between operations: 16.3 us -> 1.31 us
  other arithmetic: 4.13 us -> 0 us
  local copies, waits for them, and re-layouts: 9.43 us -> 5.74 us
    reduce_scatter x1 -> x0, waiting for transfers between devices: 131 us -> none  [reduce_weights(): return lax.psum_scatter(term, 'scene', scatter_dimension=1, tiled=True)]
    pallas_call x0 -> x1, Pallas kernels: none -> 59.9 us  [fused_shards(): pl.pallas_call(functools.partial(attention_kernel, scenes), out_shape=(ja...]
    psum x1 -> x0, waiting for transfers between devices: 53.6 us -> none  [shards(): summed = lax.psum(partial_sum, ('section', 'mp')).astype(jnp.float32)]
    dot_general x7 -> x0, matrix products: 19.4 us -> none  [the longest x1 4.82 us: shards(): jnp.einsum('td,hd->th', upstream, lax.all_gather(w_out, 'scene', axis=1,...]
    all_gather x1 -> x0, waiting for transfers between devices: 17.6 us -> none  [shards(): lax.all_gather(w_out, 'scene', axis=1, tiled=True)]
    sub x1 -> x0, matrix products: 4.62 us -> none  [attend_forward(): exponent = jnp.exp(scores - largest)]
    convert_element_type x1 -> x0, other arithmetic: 3.44 us -> none  [attend_forward(): weights = probs.astype(jnp.bfloat16)]
    another operation x3 -> x0, local copies, waits for them, and re-layouts: 2.95 us -> none  [the longest x1 1.33 us: shards(): value_heads = value_rows.reshape(-1, head_count, HEAD_DIM)]
  transfers between devices with their start and end apart: 3 -> 0, of which waited for: 3 -> 0; matrix products, arithmetic and copies ran while one was open for 9% -> 0% of each run, Pallas kernels for 0% -> 0%
where the time goes in v2:
time: 67.2 us; the launch traced here: 67 us
  Pallas kernels  59.9 us (89%)
  local copies, waits for them, and re-layouts  5.74 us (9%)
  between operations  1.31 us (2%)
    pallas_call x1, Pallas kernels, fused_shards(): pl.pallas_call(functools.partial(attention_kernel, scenes), out_shape=(ja...  59.9 us
    unnamed x12, local copies, waits for them, and re-layouts  5.74 us

profile of v2, /device:TPU:0, one launch (start us, length us, event | category | flops | bytes accessed | tf_op | source)
XLA Modules:
  0.0 67.0 jit_solution(16764580327206788666)
XLA Ops:
  1.3 0.0 copy-start
  1.3 0.9 %copy-done = bf16[1,256,512]{2,1,0:T(8,128)(2,1)S(1)} copy-done((bf16[1,256,512]{2,1,0:T(8,128)(2,1)S(1)}, bf16[1,256,512]{2,1,0:T(8,128)(2,1)}, u32[]{:S(2)}) %copy-start) | copy-done | bytes 262168
  2.2 0.0 copy-start.1
  2.2 0.7 %copy-done.1 = s32[1,2,8]{2,1,0:T(2,128)S(1)} copy-done((s32[1,2,8]{2,1,0:T(2,128)S(1)}, s32[1,2,8]{2,1,0:T(2,128)}, u32[]{:S(2)}) %copy-start.1) | copy-done | bytes 88
  2.9 59.9 %shard_map.102 = (bf16[1,256,512]{2,1,0:T(8,128)(2,1)S(1)}, bf16[1,1024,512]{2,1,0:T(8,128)(2,1)S(1)}, bf16[1,1024,512]{2,1,0:T(8,128)(2,1)}, f32[512,1024]{1,0:T(8,128)}) custom-call(bf16[1,1,256,4096]{3,2,1,0:T(8,128)(2,1)} %dec_hbm.1, bf16[1,256,512]{2,1,0:T(8,128)(2,1)S(1)} %copy-done, bf16[1,1024,512]{2,1,0:T(8,128)(2,1)} %k_hbm.1, ...), custom_call_target="tpu_custom_call" | custom-call | tf_op jit(solution)/shard_map/pallas_call | solution.py:463
  62.9 0.0 copy-start.3
  62.9 0.7 %copy.16 = bf16[1,256,512]{2,1,0:T(8,128)(2,1)} copy(bf16[1,256,512]{2,1,0:T(8,128)(2,1)S(1)} %get-tuple-element.8) | data formatting | bytes 524288
  63.6 0.0 copy-start.2
  63.6 1.0 %copy.17 = bf16[1,1024,512]{2,1,0:T(8,128)(2,1)} copy(bf16[1,1024,512]{2,1,0:T(8,128)(2,1)S(1)} %get-tuple-element.9) | data formatting | bytes 2097152
  64.5 0.0 copy-done.3
  64.5 1.0 %copy.18 = bf16[1,1024,512]{2,1,0:T(8,128)(2,1)} copy(bf16[1,1024,512]{2,1,0:T(8,128)(2,1)S(1)} %copy-done.3) | data formatting | bytes 2097152
  65.5 0.1 copy-done.2
  65.7 1.3 %copy.19 = f32[512,1024]{1,0:T(8,128)} copy(f32[512,1024]{1,0:T(8,128)S(1)} %copy-done.2) | data formatting | bytes 4194304
Async XLA Ops:
  1.3 1.0 %copy-start = (bf16[1,256,512]{2,1,0:T(8,128)(2,1)S(1)}, bf16[1,256,512]{2,1,0:T(8,128)(2,1)}, u32[]{:S(2)}) copy-start(bf16[1,256,512]{2,1,0:T(8,128)(2,1)} %q_hbm.1) | copy-start | bytes 786436
  2.2 0.7 %copy-start.1 = (s32[1,2,8]{2,1,0:T(2,128)S(1)}, s32[1,2,8]{2,1,0:T(2,128)}, u32[]{:S(2)}) copy-start(s32[1,2,8]{2,1,0:T(2,128)} %mask_ref.1) | copy-start | bytes 196
  62.9 1.7 %copy-start.3 = (bf16[1,1024,512]{2,1,0:T(8,128)(2,1)S(1)}, bf16[1,1024,512]{2,1,0:T(8,128)(2,1)}, u32[]{:S(2)}) copy-start(bf16[1,1024,512]{2,1,0:T(8,128)(2,1)} %get-tuple-element.10) | copy-start | bytes 3145732
  63.6 2.1 %copy-start.2 = (f32[512,1024]{1,0:T(8,128)S(1)}, f32[512,1024]{1,0:T(8,128)}, u32[]{:S(2)}) copy-start(f32[512,1024]{1,0:T(8,128)} %get-tuple-element.11) | copy-start | bytes 6291460

commit v3 on v2

--- a/solution.py
+++ b/solution.py
@@ -98,8 +98,8 @@
     scenes, dec_hbm, q_hbm, k_hbm, v_hbm, w_hbm, mask_ref, count_ref,
     dq_hbm, dk_hbm, dv_hbm, dw_hbm,
     dec_ref, q_ref, k_ref, v_ref, w_ref, dq_ref, dk_ref, dv_ref, dw_ref,
-    core_in, acc, half_in, acc_half, quarter_in, piece, up, att_all, attended, probs,
-    parts, part_out, part_in, part_own, grads,
+    core_in, acc, half_in, acc_half, quarter_in, piece, up, att_all, keys_t, probs,
+    parts, part_out, part_in,
     load_sem, store_sem, core_send, core_recv, half_send, half_recv, quarter_send, quarter_recv,
     swap_send, swap_recv, g1_send, g1_recv, g2_send, g2_recv,
     g3_send, g3_recv, att_send, att_recv, part_send, part_recv,
@@ -159,31 +159,38 @@
     for j in range(scenes):
         core_copy(j).start()
 
-    def forward(h, carry):
-        head = span(h * HEAD_DIM, HEAD_DIM)
-        for qb in range(q_blocks):
-            block = pl.ds(qb * q_block, q_block)
-            scores = lax.dot_general(
-                q_ref[0, block, head], k_ref[0, :, head], (((1,), (1,)), ((), ())),
-                preferred_element_type=jnp.float32,
-            ) * scaling
-            hidden = jnp.concatenate(
-                [
-                    jnp.full((1, map_block), jnp.where(mask_ref[0, qb, mb] == 1, 0.0, -1e30), jnp.float32)
-                    for mb in range(map_blocks)
-                ],
-                axis=1,
-            )
-            scores = scores + hidden
-            exponent = jnp.exp(scores - jnp.max(scores, axis=-1, keepdims=True))
-            prob = exponent / jnp.sum(exponent, axis=-1, keepdims=True)
-            probs[h, block, :] = prob
-            value = jnp.dot(
-                prob.astype(jnp.bfloat16), v_ref[0, :, head], preferred_element_type=jnp.float32
-            )
-            attended[block, head] = value
-            att_all[z, block, head] = value.astype(jnp.bfloat16)
-        return carry
+    def forward(h):
+        head = slice(h * HEAD_DIM, (h + 1) * HEAD_DIM)
+        hidden = jnp.concatenate(
+            [
+                jnp.concatenate(
+                    [
+                        jnp.full(
+                            (map_block, q_block),
+                            jnp.where(mask_ref[0, qb, mb] == 1, 0.0, -1e30),
+                            jnp.float32,
+                        )
+                        for qb in range(q_blocks)
+                    ],
+                    axis=1,
+                )
+                for mb in range(map_blocks)
+            ],
+            axis=0,
+        )
+        scores = hidden + scaling * lax.dot_general(
+            k_ref[0, :, head], q_ref[0, :, head], (((1,), (1,)), ((), ())),
+            preferred_element_type=jnp.float32,
+        )
+        exponent = jnp.exp(scores - jnp.max(scores, axis=0, keepdims=True))
+        prob = exponent * (1.0 / jnp.sum(exponent, axis=0, keepdims=True))
+        probs[h] = prob
+        value = lax.dot_general(
+            v_ref[0, :, head], prob.astype(jnp.bfloat16), (((0,), (0,)), ((), ())),
+            preferred_element_type=jnp.float32,
+        )
+        att_all[z, :, head] = value.T.astype(jnp.bfloat16)
+        keys_t[h] = k_ref[0, :, head].T
 
     def add(a, b):
         return (a.astype(jnp.float32) + b.astype(jnp.float32)).astype(jnp.bfloat16)
@@ -290,48 +297,52 @@
             gather_two(j, l, 1).wait_recv()
         gather_three(j).start()
 
-    def part_copy(j):
+    def part_copy(j, b):
         t = targets[j]
         to = z + jnp.where(t > z, 1, -1)
         slot = jnp.where(jnp.logical_and(to == t, t < z), scenes, t)
         return remote(
-            part_out.at[j], part_in.at[slot], part_send.at[j], part_recv.at[slot], {"scene": to}
-        )
-
-    def landed_part(slot):
+            part_out.at[j, b], part_in.at[slot, b], part_send.at[j, b], part_recv.at[slot, b],
+            {"scene": to},
+        )
+
+    def landed_part(slot, b):
         return remote(
-            part_out.at[0], part_in.at[slot], part_send.at[0], part_recv.at[slot], core_peer
-        )
-
-    inner = jnp.logical_and(z > 0, z < scenes - 1)
+            part_out.at[0, b], part_in.at[slot, b], part_send.at[0, b], part_recv.at[slot, b],
+            core_peer,
+        )
+
+    share = width // 2
     has_prev = [jnp.where(targets[j] > z, z, scenes - 1 - z) > 0 for j in range(scenes)]
 
     def multiply(j):
         gather_three(j, 1).wait_recv()
         t = targets[j]
-        part = sum(
-            lax.dot_general(
-                up[t, l], w_ref[:, l * lane : (l + 1) * lane], (((1,), (1,)), ((), ())),
-                preferred_element_type=jnp.float32,
+        for b in range(2):
+            part = sum(
+                lax.dot_general(
+                    up[t, l],
+                    w_ref[b * share : (b + 1) * share, l * lane : (l + 1) * lane],
+                    (((1,), (1,)), ((), ())),
+                    preferred_element_type=jnp.float32,
+                )
+                for l in range(2)
             )
-            for l in range(2)
-        )
-        if j == scenes - 1:
-            part_own[...] = part
-            return
-        parts[j] = part
-
-        @pl.when(jnp.logical_not(has_prev[j]))
-        def _():
-            part_out[j] = parts[j].astype(jnp.bfloat16)
-            part_copy(j).start()
+            parts[j, b] = part
+            if j < scenes - 1:
+
+                @pl.when(jnp.logical_not(has_prev[j]))
+                def _():
+                    part_out[j, b] = parts[j, b].astype(jnp.bfloat16)
+                    part_copy(j, b).start()
 
     def merge(j):
         @pl.when(has_prev[j])
         def _():
-            landed_part(targets[j]).wait_recv()
-            part_out[j] = (parts[j] + part_in[targets[j]].astype(jnp.float32)).astype(jnp.bfloat16)
-            part_copy(j).start()
+            for b in range(2):
+                landed_part(targets[j], b).wait_recv()
+                part_out[j, b] = add(parts[j, b], part_in[targets[j], b])
+                part_copy(j, b).start()
 
     stages = (
         sum_core, sum_half, sum_quarter, spread_one, spread_two, spread_three, multiply
@@ -339,7 +350,7 @@
     loads[0].wait()
     loads[1].wait()
     loads[2].wait()
-    forward(0, 0)
+    forward(0)
     loads[4].wait()
     for tick in range(scenes + len(stages) - 1):
         for lag, stage in enumerate(stages):
@@ -348,7 +359,7 @@
             if 0 <= tick - lag < scenes:
                 stage(tick - lag)
         if tick + 1 < heads:
-            forward(tick + 1, 0)
+            forward(tick + 1)
         if tick == heads - 2:
             move_attended(0, False)
         if tick == 5:
@@ -359,6 +370,7 @@
             merge(1)
         if tick == 9:
             merge(0)
+    merge(2)
     move_attended(scenes - 1, False)
 
     def weight_columns(tile, carry):
@@ -378,19 +390,19 @@
 
     store_dw = pltpu.make_async_copy(dw_ref, dw_hbm, store_sem.at[0])
     store_dw.start()
-    merge(2)
-
-    @pl.when(z > 0)
-    def _():
-        landed_part(z).wait_recv()
-        part_own[...] = part_own[...] + part_in[z].astype(jnp.float32)
-
-    @pl.when(z < scenes - 1)
-    def _():
-        landed_part(scenes).wait_recv()
-        part_own[...] = part_own[...] + part_in[scenes].astype(jnp.float32)
-
-    grads[...] = part_own[...].astype(jnp.bfloat16)
+
+    def finish(b):
+        own = scenes - 1
+
+        @pl.when(z > 0)
+        def _():
+            landed_part(z, b).wait_recv()
+            parts[own, b] = parts[own, b] + part_in[z, b].astype(jnp.float32)
+
+        @pl.when(z < scenes - 1)
+        def _():
+            landed_part(scenes, b).wait_recv()
+            parts[own, b] = parts[own, b] + part_in[scenes, b].astype(jnp.float32)
 
     def stores(h):
         head = span(h * HEAD_DIM, HEAD_DIM)
@@ -399,34 +411,30 @@
             for i, (src, dst) in enumerate(((dq_ref, dq_hbm), (dk_ref, dk_hbm), (dv_ref, dv_hbm)))
         ]
 
-    def backward(h, carry):
-        head = span(h * HEAD_DIM, HEAD_DIM)
-        grad = grads[:, head]
+    def backward(h):
+        head = slice(h * HEAD_DIM, (h + 1) * HEAD_DIM)
+        b, first = h * HEAD_DIM // share, h * HEAD_DIM % share
+        grad = parts[scenes - 1, b, :, first : first + HEAD_DIM].astype(jnp.bfloat16)
         prob = probs[h]
-        delta = jnp.sum(grad.astype(jnp.float32) * attended[:, head], axis=-1, keepdims=True)
-        dv_ref[0, :, head] = lax.dot_general(
-            prob.astype(jnp.bfloat16), grad, (((0,), (0,)), ((), ())),
-            preferred_element_type=jnp.float32,
+        weights = prob.astype(jnp.bfloat16)
+        dv_ref[0, :, head] = jnp.dot(
+            weights, grad, preferred_element_type=jnp.float32
         ).astype(jnp.bfloat16)
         d_probs = lax.dot_general(
-            grad, v_ref[0, :, head], (((1,), (1,)), ((), ())), preferred_element_type=jnp.float32
-        )
+            v_ref[0, :, head], grad, (((1,), (1,)), ((), ())), preferred_element_type=jnp.float32
+        )
+        delta = jnp.sum(weights.astype(jnp.float32) * d_probs, axis=0, keepdims=True)
         score_grads = (prob * (d_probs - delta)).astype(jnp.bfloat16)
-        dq_ref[0, :, head] = (
-            scaling
-            * jnp.dot(score_grads, k_ref[0, :, head], preferred_element_type=jnp.float32)
+        dk_ref[0, :, head] = (
+            scaling * jnp.dot(score_grads, q_ref[0, :, head], preferred_element_type=jnp.float32)
         ).astype(jnp.bfloat16)
-        dk_ref[0, :, head] = (
-            scaling
-            * lax.dot_general(
-                score_grads, q_ref[0, :, head], (((0,), (0,)), ((), ())),
-                preferred_element_type=jnp.float32,
-            )
-        ).astype(jnp.bfloat16)
-        return carry
+        d_query = scaling * jnp.dot(keys_t[h], score_grads, preferred_element_type=jnp.float32)
+        dq_ref[0, :, head] = d_query.T.astype(jnp.bfloat16)
 
     for h in range(heads):
-        backward(h, 0)
+        if h * HEAD_DIM % share == 0:
+            finish(h * HEAD_DIM // share)
+        backward(h)
         for store in stores(h):
             store.start()
 
@@ -443,7 +451,8 @@
                 swap(j, l, z).wait_send()
         gather_three(j).wait_send()
         if j < scenes - 1:
-            part_copy(j).wait_send()
+            for b in range(2):
+                part_copy(j, b).wait_send()
     store_dw.wait()
     for h in range(heads):
         for store in stores(h):
@@ -458,7 +467,7 @@
     lane = cols // 2
     heads = width // HEAD_DIM
     bf16, f32 = jnp.bfloat16, jnp.float32
-    anywhere, smem = pl.BlockSpec(memory_space=pl.ANY), pl.BlockSpec(memory_space=pltpu.SMEM)
+    anywhere, smem = pl.BlockSpec(memory_space=pltpu.HBM), pl.BlockSpec(memory_space=pltpu.SMEM)
     dma, vmem = pltpu.SemaphoreType.DMA, pltpu.VMEM
     return pl.pallas_call(
         functools.partial(attention_kernel, scenes),
@@ -488,13 +497,11 @@
             vmem((scenes, 2, rows // 8, lane), bf16),
             vmem((scenes, 2, rows, lane), bf16),
             vmem((scenes, rows, width), bf16),
-            vmem((rows, width), f32),
-            vmem((heads, rows, map_rows), f32),
-            vmem((scenes, rows, width), f32),
-            vmem((scenes, rows, width), bf16),
-            vmem((scenes + 1, rows, width), bf16),
-            vmem((rows, width), f32),
-            vmem((rows, width), bf16),
+            vmem((heads, HEAD_DIM, map_rows), bf16),
+            vmem((heads, map_rows, rows), f32),
+            vmem((scenes, 2, rows, width // 2), f32),
+            vmem((scenes, 2, rows, width // 2), bf16),
+            vmem((scenes + 1, 2, rows, width // 2), bf16),
             dma((5,)),
             dma((1 + 3 * heads,)),
             dma((scenes,)),
@@ -504,8 +511,8 @@
             dma((scenes,)),
             dma((2, scenes)),
             dma((scenes,)),
-            dma((scenes,)),
-            dma((scenes + 1,)),
+            dma((scenes, 2)),
+            dma((scenes + 1, 2)),
         ],
         compiler_params=pltpu.CompilerParams(
             collective_id=0, has_side_effects=True, vmem_limit_bytes=52 * 1024 * 1024
@@ -523,6 +530,7 @@
             and scenes == 4
             and dec_grad.shape[2] % 128 == 0
             and w_out.shape[1] % 512 == 0
+            and w_out.shape[0] % 256 == 0
         )
         return functools.partial(fused_shards, scenes)(*args) if fits else shards(*args)
 

time: 67.2 us -> 64.3 us (0.957)
  Pallas kernels: 59.9 us -> 57.1 us
    pallas_call x1, Pallas kernels: 59.9 us -> 57.1 us  [fused_shards(): pl.pallas_call(functools.partial(attention_kernel, scenes), out_shape=(ja...]
where the time goes in v3:
time: 64.3 us; the launch traced here: 64.1 us
  Pallas kernels  57.1 us (89%)
  local copies, waits for them, and re-layouts  5.74 us (9%)
  between operations  1.31 us (2%)
    pallas_call x1, Pallas kernels, fused_shards(): pl.pallas_call(functools.partial(attention_kernel, scenes), out_shape=(ja...  57.1 us
    unnamed x12, local copies, waits for them, and re-layouts  5.74 us

profile of v3, /device:TPU:0, one launch (start us, length us, event | category | flops | bytes accessed | tf_op | source)
XLA Modules:
  0.0 64.1 jit_solution(3830033023942618122)
XLA Ops:
  1.3 0.0 copy-start
  1.3 0.9 %copy-done = bf16[1,256,512]{2,1,0:T(8,128)(2,1)S(1)} copy-done((bf16[1,256,512]{2,1,0:T(8,128)(2,1)S(1)}, bf16[1,256,512]{2,1,0:T(8,128)(2,1)}, u32[]{:S(2)}) %copy-start) | copy-done | bytes 262168
  2.2 0.0 copy-start.1
  2.2 0.7 %copy-done.1 = s32[1,2,8]{2,1,0:T(2,128)S(1)} copy-done((s32[1,2,8]{2,1,0:T(2,128)S(1)}, s32[1,2,8]{2,1,0:T(2,128)}, u32[]{:S(2)}) %copy-start.1) | copy-done | bytes 88
  2.9 57.1 %shard_map.102 = (bf16[1,256,512]{2,1,0:T(8,128)(2,1)S(1)}, bf16[1,1024,512]{2,1,0:T(8,128)(2,1)S(1)}, bf16[1,1024,512]{2,1,0:T(8,128)(2,1)}, f32[512,1024]{1,0:T(8,128)}) custom-call(bf16[1,1,256,4096]{3,2,1,0:T(8,128)(2,1)} %dec_hbm.1, bf16[1,256,512]{2,1,0:T(8,128)(2,1)S(1)} %copy-done, bf16[1,1024,512]{2,1,0:T(8,128)(2,1)} %k_hbm.1, ...), custom_call_target="tpu_custom_call" | custom-call | tf_op jit(solution)/shard_map/pallas_call | solution.py:472
  60.0 0.0 copy-start.3
  60.0 0.7 %copy.16 = bf16[1,256,512]{2,1,0:T(8,128)(2,1)} copy(bf16[1,256,512]{2,1,0:T(8,128)(2,1)S(1)} %get-tuple-element.8) | data formatting | bytes 524288
  60.7 0.0 copy-start.2
  60.7 1.0 %copy.17 = bf16[1,1024,512]{2,1,0:T(8,128)(2,1)} copy(bf16[1,1024,512]{2,1,0:T(8,128)(2,1)S(1)} %get-tuple-element.9) | data formatting | bytes 2097152
  61.7 0.0 copy-done.3
  61.7 1.0 %copy.18 = bf16[1,1024,512]{2,1,0:T(8,128)(2,1)} copy(bf16[1,1024,512]{2,1,0:T(8,128)(2,1)S(1)} %copy-done.3) | data formatting | bytes 2097152
  62.7 0.1 copy-done.2
  62.8 1.3 %copy.19 = f32[512,1024]{1,0:T(8,128)} copy(f32[512,1024]{1,0:T(8,128)S(1)} %copy-done.2) | data formatting | bytes 4194304
Async XLA Ops:
  1.3 1.0 %copy-start = (bf16[1,256,512]{2,1,0:T(8,128)(2,1)S(1)}, bf16[1,256,512]{2,1,0:T(8,128)(2,1)}, u32[]{:S(2)}) copy-start(bf16[1,256,512]{2,1,0:T(8,128)(2,1)} %q_hbm.1) | copy-start | bytes 786436
  2.2 0.7 %copy-start.1 = (s32[1,2,8]{2,1,0:T(2,128)S(1)}, s32[1,2,8]{2,1,0:T(2,128)}, u32[]{:S(2)}) copy-start(s32[1,2,8]{2,1,0:T(2,128)} %mask_ref.1) | copy-start | bytes 196
  60.0 1.7 %copy-start.3 = (bf16[1,1024,512]{2,1,0:T(8,128)(2,1)S(1)}, bf16[1,1024,512]{2,1,0:T(8,128)(2,1)}, u32[]{:S(2)}) copy-start(bf16[1,1024,512]{2,1,0:T(8,128)(2,1)} %get-tuple-element.10) | copy-start | bytes 3145732
  60.7 2.1 %copy-start.2 = (f32[512,1024]{1,0:T(8,128)S(1)}, f32[512,1024]{1,0:T(8,128)}, u32[]{:S(2)}) copy-start(f32[512,1024]{1,0:T(8,128)} %get-tuple-element.11) | copy-start | bytes 6291460

commit v4 on v3

--- a/solution.py
+++ b/solution.py
@@ -98,19 +98,21 @@
     scenes, dec_hbm, q_hbm, k_hbm, v_hbm, w_hbm, mask_ref, count_ref,
     dq_hbm, dk_hbm, dv_hbm, dw_hbm,
     dec_ref, q_ref, k_ref, v_ref, w_ref, dq_ref, dk_ref, dv_ref, dw_ref,
-    core_in, acc, half_in, acc_half, quarter_in, piece, up, att_all, keys_t, probs,
-    parts, part_out, part_in,
-    load_sem, store_sem, core_send, core_recv, half_send, half_recv, quarter_send, quarter_recv,
-    swap_send, swap_recv, g1_send, g1_recv, g2_send, g2_recv,
-    g3_send, g3_recv, att_send, att_recv, part_send, part_recv,
+    core_in, acc, plane_in, piece, up, att_all, keys_t, probs, parts, part_out, part_in,
+    load_sem, store_sem, core_send, core_recv, plane_send, plane_recv, swap_send, swap_recv,
+    gather_send, gather_recv, share_send, share_recv, att_send, att_recv, part_send, part_recv,
 ):
     z, y, m = lax.axis_index("scene"), lax.axis_index("section"), lax.axis_index("mp")
     x, c = lax.div(m, 2), lax.rem(m, 2)
-    core_peer, x_peer, y_peer = {"mp": m + 1 - 2 * c}, {"mp": m + 2 - 4 * x}, {"section": 1 - y}
+    core_peer = {"mp": m + 1 - 2 * c}
+    chips = [
+        {"section": 1 - y if i & 2 else y, "mp": m + 2 - 4 * x if i & 1 else m} for i in range(4)
+    ]
+    chip = 2 * y + x
+    rows_of = [2 * (1 - y if i & 2 else y) + (1 - x if i & 1 else x) for i in range(4)]
     rows, width = q_ref.shape[1], q_ref.shape[2]
-    half, quarter, eighth = rows // 2, rows // 4, rows // 8
+    half, eighth = rows // 2, rows // 8
     cols = w_ref.shape[1]
-    lane = cols // 2
     heads = width // HEAD_DIM
     scaling = 1.0 / math.sqrt(HEAD_DIM)
     map_blocks, q_blocks = mask_ref.shape[2], mask_ref.shape[1]
@@ -145,7 +147,7 @@
         load.start()
 
     barrier = pltpu.get_barrier_semaphore()
-    peers = [core_peer, x_peer, y_peer] + [{"scene": targets[j]} for j in range(scenes - 1)]
+    peers = [core_peer] + chips[1:] + [{"scene": targets[j]} for j in range(scenes - 1)]
     for peer in peers:
         pl.semaphore_signal(barrier, inc=1, device_id=peer, device_id_type=pl.DeviceIdType.MESH)
     pl.semaphore_wait(barrier, len(peers))
@@ -156,8 +158,7 @@
             core_in.at[j], core_send.at[j], core_recv.at[j], core_peer,
         )
 
-    for j in range(scenes):
-        core_copy(j).start()
+    core_copy(0).start()
 
     def forward(h):
         head = slice(h * HEAD_DIM, (h + 1) * HEAD_DIM)
@@ -215,87 +216,60 @@
                     copy.wait_recv()
                     pl.when(onward)(lambda: copy.start())
 
-    bits = ((x, y), (y, x))
-    order = ((x_peer, y_peer), (y_peer, x_peer))
-    starts = [c * half + bits[l][0] * quarter + bits[l][1] * eighth for l in range(2)]
-    places = [span(starts[l], eighth) for l in range(2)]
-
-    def half_copy(j, l):
+    my_rows = span(c * half + chip * eighth, eighth)
+
+    def plane_copy(j, i):
         return remote(
-            acc.at[j, l, span((1 - bits[l][0]) * quarter, quarter), :], half_in.at[j, l],
-            half_send.at[j, l], half_recv.at[j, l], order[l][0],
-        )
-
-    def quarter_copy(j, l):
+            acc.at[j, span(rows_of[i] * eighth, eighth), :], plane_in.at[j, i],
+            plane_send.at[j, i], plane_recv.at[j, i], chips[i],
+        )
+
+    def swap(j, slot):
         return remote(
-            acc_half.at[j, l, span((1 - bits[l][1]) * eighth, eighth), :], quarter_in.at[j, l],
-            quarter_send.at[j, l], quarter_recv.at[j, l], order[l][1],
-        )
-
-    def swap(j, l, slot):
-        return remote(
-            piece.at[j, l], up.at[slot, l, places[l], :], swap_send.at[j, l], swap_recv.at[j, l],
+            piece.at[j], up.at[slot, my_rows, :], swap_send.at[j], swap_recv.at[j],
             {"scene": targets[j]},
         )
 
     def sum_core(j):
+        if j + 1 < scenes:
+            core_copy(j + 1).start()
         core_copy(j).wait_recv()
-        for l in range(2):
-            mine = dec_ref[:, span(targets[j] * cols + l * lane, lane)]
-            acc[j, l] = add(mine, core_in[j, :, l * lane : (l + 1) * lane])
-            half_copy(j, l).start()
-
-    def sum_half(j):
-        for l in range(2):
-            half_copy(j, l).wait_recv()
-            acc_half[j, l] = add(acc[j, l, span(bits[l][0] * quarter, quarter), :], half_in[j, l])
-            quarter_copy(j, l).start()
-
-    def sum_quarter(j):
-        for l in range(2):
-            quarter_copy(j, l).wait_recv()
-            total = add(acc_half[j, l, span(bits[l][1] * eighth, eighth), :], quarter_in[j, l])
-            row = starts[l] + lax.broadcasted_iota(jnp.int32, total.shape, 0)
-            total = jnp.where(row < count_ref[0], total.astype(jnp.float32), 0.0)
-            if j < scenes - 1:
-                piece[j, l] = total.astype(jnp.bfloat16)
-                swap(j, l, z).start()
-            else:
-                up[z, l, places[l], :] = total.astype(jnp.bfloat16)
-
-    def gathered(j, l, size, lead, sems, peer):
-        ref = up.at[targets[j], l, span(lead, size), :]
-        return remote(ref, ref, sems[0].at[j, l], sems[1].at[j, l], peer)
-
-    def gather_one(j, l, away=0):
-        bit = 1 - bits[l][1] if away else bits[l][1]
-        lead = c * half + bits[l][0] * quarter + bit * eighth
-        return gathered(j, l, eighth, lead, (g1_send, g1_recv), order[l][1])
-
-    def gather_two(j, l, away=0):
-        bit = 1 - bits[l][0] if away else bits[l][0]
-        return gathered(j, l, quarter, c * half + bit * quarter, (g2_send, g2_recv), order[l][0])
-
-    def gather_three(j, away=0):
-        core = 1 - c if away else c
-        ref = up.at[targets[j], :, span(core * half, half), :]
-        return remote(ref, ref, g3_send.at[j], g3_recv.at[j], core_peer)
-
-    def spread_one(j):
-        for l in range(2):
-            if j < scenes - 1:
-                swap(j, l, targets[j]).wait_recv()
-            gather_one(j, l).start()
-
-    def spread_two(j):
-        for l in range(2):
-            gather_one(j, l, 1).wait_recv()
-            gather_two(j, l).start()
-
-    def spread_three(j):
-        for l in range(2):
-            gather_two(j, l, 1).wait_recv()
-        gather_three(j).start()
+        acc[j] = add(dec_ref[:, span(targets[j] * cols, cols)], core_in[j])
+        for i in range(1, 4):
+            plane_copy(j, i).start()
+
+    def sum_plane(j):
+        total = acc[j, span(chip * eighth, eighth), :].astype(jnp.float32)
+        for i in range(1, 4):
+            plane_copy(j, i).wait_recv()
+            total = total + plane_in[j, i].astype(jnp.float32)
+        row = c * half + chip * eighth + lax.broadcasted_iota(jnp.int32, total.shape, 0)
+        total = jnp.where(row < count_ref[0], total, 0.0).astype(jnp.bfloat16)
+        if j < scenes - 1:
+            piece[j] = total
+            swap(j, z).start()
+        else:
+            up[z, my_rows, :] = total
+
+    def gather(j, i, away=0):
+        part_rows = span(c * half + rows_of[i if away else 0] * eighth, eighth)
+        ref = up.at[targets[j], part_rows, :]
+        return remote(ref, ref, gather_send.at[j, i], gather_recv.at[j, i], chips[i])
+
+    def share_core(j, away=0):
+        ref = up.at[targets[j], span((1 - c if away else c) * half, half), :]
+        return remote(ref, ref, share_send.at[j], share_recv.at[j], core_peer)
+
+    def spread_plane(j):
+        if j < scenes - 1:
+            swap(j, targets[j]).wait_recv()
+        for i in range(1, 4):
+            gather(j, i).start()
+
+    def spread_core(j):
+        for i in range(1, 4):
+            gather(j, i, 1).wait_recv()
+        share_core(j).start()
 
     def part_copy(j, b):
         t = targets[j]
@@ -312,44 +286,36 @@
             core_peer,
         )
 
-    share = width // 2
     has_prev = [jnp.where(targets[j] > z, z, scenes - 1 - z) > 0 for j in range(scenes)]
 
     def multiply(j):
-        gather_three(j, 1).wait_recv()
-        t = targets[j]
-        for b in range(2):
-            part = sum(
-                lax.dot_general(
-                    up[t, l],
-                    w_ref[b * share : (b + 1) * share, l * lane : (l + 1) * lane],
-                    (((1,), (1,)), ((), ())),
-                    preferred_element_type=jnp.float32,
-                )
-                for l in range(2)
+        share_core(j, 1).wait_recv()
+        for two in range(0, heads, 2):
+            part = lax.dot_general(
+                up[targets[j]], w_ref[two * HEAD_DIM : (two + 2) * HEAD_DIM, :],
+                (((1,), (1,)), ((), ())), preferred_element_type=jnp.float32,
             )
-            parts[j, b] = part
+            for b in (two, two + 1):
+                parts[j, b] = part[:, (b - two) * HEAD_DIM : (b - two + 1) * HEAD_DIM]
             if j < scenes - 1:
 
                 @pl.when(jnp.logical_not(has_prev[j]))
                 def _():
-                    part_out[j, b] = parts[j, b].astype(jnp.bfloat16)
-                    part_copy(j, b).start()
+                    for b in (two, two + 1):
+                        part_out[j, b] = parts[j, b].astype(jnp.bfloat16)
+                        part_copy(j, b).start()
 
     def merge(j):
         @pl.when(has_prev[j])
         def _():
-            for b in range(2):
+            for b in range(heads):
                 landed_part(targets[j], b).wait_recv()
                 part_out[j, b] = add(parts[j, b], part_in[targets[j], b])
                 part_copy(j, b).start()
 
-    stages = (
-        sum_core, sum_half, sum_quarter, spread_one, spread_two, spread_three, multiply
-    )
-    loads[0].wait()
-    loads[1].wait()
-    loads[2].wait()
+    stages = (sum_core, sum_plane, spread_plane, spread_core, multiply)
+    for load in loads[:3]:
+        load.wait()
     forward(0)
     loads[4].wait()
     for tick in range(scenes + len(stages) - 1):
@@ -358,35 +324,33 @@
                 loads[3].wait()
             if 0 <= tick - lag < scenes:
                 stage(tick - lag)
-        if tick + 1 < heads:
-            forward(tick + 1)
-        if tick == heads - 2:
+        if tick == 0:
+            forward(1)
+        if tick == 1:
+            for h in range(2, heads):
+                forward(h)
             move_attended(0, False)
-        if tick == 5:
+        if tick == 4:
             move_attended(1, False)
-        if tick == 7:
+        if tick == 6:
             move_attended(2, False)
-        if tick == 8:
             merge(1)
-        if tick == 9:
-            merge(0)
+    merge(0)
     merge(2)
     move_attended(scenes - 1, False)
 
     def weight_columns(tile, carry):
-        for l in range(2):
-            size = lane // 2
-            at = span(tile * size, size)
-            dw_ref[:, span(l * lane + tile * size, size)] = sum(
-                lax.dot_general(
-                    att_all[s], up[s, l, :, at], (((0,), (0,)), ((), ())),
-                    preferred_element_type=jnp.float32,
-                )
-                for s in range(scenes)
+        at = span(tile * 256, 256)
+        dw_ref[:, at] = sum(
+            lax.dot_general(
+                att_all[s], up[s, :, at], (((0,), (0,)), ((), ())),
+                preferred_element_type=jnp.float32,
             )
+            for s in range(scenes)
+        )
         return carry
 
-    lax.fori_loop(0, 2, weight_columns, 0)
+    lax.fori_loop(0, cols // 256, weight_columns, 0)
 
     store_dw = pltpu.make_async_copy(dw_ref, dw_hbm, store_sem.at[0])
     store_dw.start()
@@ -413,8 +377,7 @@
 
     def backward(h):
         head = slice(h * HEAD_DIM, (h + 1) * HEAD_DIM)
-        b, first = h * HEAD_DIM // share, h * HEAD_DIM % share
-        grad = parts[scenes - 1, b, :, first : first + HEAD_DIM].astype(jnp.bfloat16)
+        grad = parts[scenes - 1, h].astype(jnp.bfloat16)
         prob = probs[h]
         weights = prob.astype(jnp.bfloat16)
         dv_ref[0, :, head] = jnp.dot(
@@ -432,8 +395,7 @@
         dq_ref[0, :, head] = d_query.T.astype(jnp.bfloat16)
 
     for h in range(heads):
-        if h * HEAD_DIM % share == 0:
-            finish(h * HEAD_DIM // share)
+        finish(h)
         backward(h)
         for store in stores(h):
             store.start()
@@ -442,16 +404,14 @@
         move_attended(step, True)
     for j in range(scenes):
         core_copy(j).wait_send()
-        for l in range(2):
-            half_copy(j, l).wait_send()
-            quarter_copy(j, l).wait_send()
-            gather_one(j, l).wait_send()
-            gather_two(j, l).wait_send()
-            if j < scenes - 1:
-                swap(j, l, z).wait_send()
-        gather_three(j).wait_send()
+        for i in range(1, 4):
+            plane_copy(j, i).wait_send()
+            gather(j, i).wait_send()
+        share_core(j).wait_send()
         if j < scenes - 1:
-            for b in range(2):
+            swap(j, z).wait_send()
+        if j < scenes - 1:
+            for b in range(heads):
                 part_copy(j, b).wait_send()
     store_dw.wait()
     for h in range(heads):
@@ -464,7 +424,6 @@
     map_rows = map_keys.shape[1]
     model = dec_grad.shape[3]
     cols = w_out.shape[1]
-    lane = cols // 2
     heads = width // HEAD_DIM
     bf16, f32 = jnp.bfloat16, jnp.float32
     anywhere, smem = pl.BlockSpec(memory_space=pltpu.HBM), pl.BlockSpec(memory_space=pltpu.SMEM)
@@ -490,32 +449,31 @@
             vmem((1, map_rows, width), bf16),
             vmem((width, cols), f32),
             vmem((scenes, rows // 2, cols), bf16),
-            vmem((scenes, 2, rows // 2, lane), bf16),
-            vmem((scenes, 2, rows // 4, lane), bf16),
-            vmem((scenes, 2, rows // 4, lane), bf16),
-            vmem((scenes, 2, rows // 8, lane), bf16),
-            vmem((scenes, 2, rows // 8, lane), bf16),
-            vmem((scenes, 2, rows, lane), bf16),
+            vmem((scenes, rows // 2, cols), bf16),
+            vmem((scenes, 4, rows // 8, cols), bf16),
+            vmem((scenes, rows // 8, cols), bf16),
+            vmem((scenes, rows, cols), bf16),
             vmem((scenes, rows, width), bf16),
             vmem((heads, HEAD_DIM, map_rows), bf16),
             vmem((heads, map_rows, rows), f32),
-            vmem((scenes, 2, rows, width // 2), f32),
-            vmem((scenes, 2, rows, width // 2), bf16),
-            vmem((scenes + 1, 2, rows, width // 2), bf16),
+            vmem((scenes, heads, rows, HEAD_DIM), f32),
+            vmem((scenes, heads, rows, HEAD_DIM), bf16),
+            vmem((scenes + 1, heads, rows, HEAD_DIM), bf16),
             dma((5,)),
             dma((1 + 3 * heads,)),
             dma((scenes,)),
             dma((scenes,)),
-            *[dma((scenes, 2))] * 10,
-            dma((scenes,)),
-            dma((scenes,)),
+            *[dma((scenes, 4))] * 2,
+            *[dma((scenes,))] * 2,
+            *[dma((scenes, 4))] * 2,
+            *[dma((scenes,))] * 2,
             dma((2, scenes)),
             dma((scenes,)),
-            dma((scenes, 2)),
-            dma((scenes + 1, 2)),
+            dma((scenes, heads)),
+            dma((scenes + 1, heads)),
         ],
         compiler_params=pltpu.CompilerParams(
-            collective_id=0, has_side_effects=True, vmem_limit_bytes=52 * 1024 * 1024
+            collective_id=0, has_side_effects=True, vmem_limit_bytes=62 * 1024 * 1024
         ),
     )(dec_grad, agent_queries, map_keys, map_values, w_out, block_mask, agent_count)
 

time: 64.3 us -> 63.6 us (0.989)
  Pallas kernels: 57.1 us -> 55.7 us
  local copies, waits for them, and re-layouts: 5.74 us -> 6.46 us
    pallas_call x1, Pallas kernels: 57.1 us -> 55.7 us  [fused_shards(): pl.pallas_call(functools.partial(attention_kernel, scenes), out_shape=(ja...]
    unnamed x12 -> x8, local copies, waits for them, and re-layouts: 5.74 us -> 6.46 us
where the time goes in v4:
time: 63.6 us; the launch traced here: 63.4 us
  Pallas kernels  55.7 us (88%)
  local copies, waits for them, and re-layouts  6.46 us (10%)
  between operations  1.3 us (2%)
    pallas_call x1, Pallas kernels, fused_shards(): pl.pallas_call(functools.partial(attention_kernel, scenes), out_shape=(ja...  55.7 us
    unnamed x8, local copies, waits for them, and re-layouts  6.46 us

profile of v4, /device:TPU:0, one launch (start us, length us, event | category | flops | bytes accessed | tf_op | source)
XLA Modules:
  0.0 63.4 jit_solution(12726324387925846210)
XLA Ops:
  1.3 55.7 %shard_map.102 = (bf16[1,256,512]{2,1,0:T(8,128)(2,1)}, bf16[1,1024,512]{2,1,0:T(8,128)(2,1)}, bf16[1,1024,512]{2,1,0:T(8,128)(2,1)}, f32[512,1024]{1,0:T(8,128)}) custom-call(bf16[1,1,256,4096]{3,2,1,0:T(8,128)(2,1)} %dec_hbm.1, bf16[1,256,512]{2,1,0:T(8,128)(2,1)} %q_hbm.1, bf16[1,1024,512]{2,1,0:T(8,128)(2,1)} %k_hbm.1, bf16[1,1024,512]{2,1,0:T(8,128)(2,1)} %v_hbm.1, ...), custom_call_target="tpu_custom_call" | custom-call | tf_op jit(solution)/shard_map/pallas_call | solution.py:431
  56.9 0.0 copy-start.1
  57.0 1.8 %copy.16 = bf16[1,256,512]{2,1,0:T(8,128)(2,1)} copy(bf16[1,256,512]{2,1,0:T(8,128)(2,1)} %get-tuple-element.8) | data formatting | bytes 524288
  58.7 0.0 copy-start
  58.7 2.4 %copy.17 = bf16[1,1024,512]{2,1,0:T(8,128)(2,1)} copy(bf16[1,1024,512]{2,1,0:T(8,128)(2,1)} %get-tuple-element.9) | data formatting | bytes 2097152
  61.1 0.0 copy-done.1
  61.1 1.0 %copy.18 = bf16[1,1024,512]{2,1,0:T(8,128)(2,1)} copy(bf16[1,1024,512]{2,1,0:T(8,128)(2,1)S(1)} %copy-done.1) | data formatting | bytes 2097152
  62.1 0.0 copy-done
  62.1 1.3 %copy.19 = f32[512,1024]{1,0:T(8,128)} copy(f32[512,1024]{1,0:T(8,128)S(1)} %copy-done) | data formatting | bytes 4194304
Async XLA Ops:
  56.9 4.2 %copy-start.1 = (bf16[1,1024,512]{2,1,0:T(8,128)(2,1)S(1)}, bf16[1,1024,512]{2,1,0:T(8,128)(2,1)}, u32[]{:S(2)}) copy-start(bf16[1,1024,512]{2,1,0:T(8,128)(2,1)} %get-tuple-element.10) | copy-start | bytes 3145732
  58.7 3.4 %copy-start = (f32[512,1024]{1,0:T(8,128)S(1)}, f32[512,1024]{1,0:T(8,128)}, u32[]{:S(2)}) copy-start(f32[512,1024]{1,0:T(8,128)} %get-tuple-element.11) | copy-start | bytes 6291460
